TPU v7x, 768 devices: a whole 4x8x12 slice. The times are simulated.
768 devices in a mesh: rep: 12 (over x, z_lo), fsdp: 64 (over z_hi, y, core).
Axes of the slice: x: 4, y: 8, z: 12 (z_hi: 4, z_lo: 3; z = z_hi * 3 + z_lo), core: 2. Of those that a mesh axis runs over, the one named last changes fastest.
Arguments:
- gate_pre: bfloat16 [6144, 12288], P('rep', 'fsdp'), may hold values from -6 to 6
- up_pre: bfloat16 [6144, 12288], P('rep', 'fsdp'), may hold values from -40 to 40
- out_grad: bfloat16 [6144, 3072], P('rep'), may hold values from -6 to 6
- inner_params: bfloat16 [12, 12288, 3072], P('rep', 'fsdp'), may hold values from -0.109375 to 0.109375
- global_params: float32 [12288, 3072], P('fsdp', 'rep'), may hold values from -0.109375 to 0.109375
- outer_momentum: float32 [12288, 3072], P('fsdp', 'rep'), may hold values from -0.15625 to 0.15625
- pair_codes: int32 [12, 12288, 1536], P('rep', 'fsdp'), may hold values from 0 to 255
- code_scales: float32 [12, 12288, 24], P('rep', 'fsdp'), may hold values from 0.001 to 0.01
Outputs:
- merged_params: bfloat16 [12, 12288, 3072], P('rep', 'fsdp')
- new_global: float32 [12288, 3072], P('fsdp', 'rep')
- new_momentum: float32 [12288, 3072], P('fsdp', 'rep')
Inputs may be any that keep to these rules, and one draw needn't show every extreme that they name: `pair_codes`: each word holds two codes of 0 to 15: its value mod 16 for column 2 j and its value // 16 for column 2 j + 1.
All inputs are finite; a program needn't handle non-finite values.
Results may differ from a plain program's by a relative error of at most 0.011.
Values may be sent and summed in bfloat16 or wider, within the bound.
No kernel may reach another device: no remote copies, remote signals or barrier semaphores. Data moves between devices by JAX's collectives and lax.ppermute only.
A program may use at most 64 MiB of HBM per device.

v0:
```python
import jax
import jax.numpy as jnp
from jax import lax
from jax.sharding import PartitionSpec as P


def outer_update(mean_delta, momentum, params):
    new_momentum = 0.9 * momentum + mean_delta
    new_global = params - 0.7 * (mean_delta + 0.9 * new_momentum)
    return (new_momentum, new_global)


def unpack(packed, scales):
    lower_code = packed % 16
    upper_code = packed // 16
    unpacked = jnp.stack([lower_code, upper_code], axis=-1).reshape(
        packed.shape[:-1] + (2 * packed.shape[-1],)
    )
    centered = (unpacked - 8).astype(jnp.float32)
    blocks = centered.reshape(packed.shape[:-1] + (scales.shape[-1], -1)) * scales[..., None]
    return blocks.reshape(unpacked.shape).astype(jnp.bfloat16)


def per_device(
    gate_pre, up_pre, out_grad, inner_params, global_params, outer_momentum, pair_codes, code_scales
):
    replicas = lax.axis_size("rep")
    tok_total = gate_pre.shape[0]
    unit_rows = gate_pre.shape[1]
    model_width = out_grad.shape[1]
    all_units = unit_rows * lax.axis_size("fsdp")
    gate_f32 = gate_pre.astype(jnp.float32)
    upper = up_pre.astype(jnp.float32)
    sigmoid_gate = jax.nn.sigmoid(gate_f32)
    hidden = (gate_f32 * sigmoid_gate * upper).astype(jnp.bfloat16)
    grads = lax.dot_general(
        hidden, out_grad, (((0,), (0,)), ((), ())), preferred_element_type=jnp.float32
    ) * (1.0 / tok_total)
    square_total = lax.psum(jnp.sum(grads * grads), "fsdp")
    root_mean = jnp.sqrt(square_total / (all_units * model_width) + 1e-06)
    clipped = grads * jnp.minimum(1.0, 0.02 / root_mean)
    pseudo = unpack(pair_codes[0], code_scales[0])
    delta_share = lax.psum_scatter(pseudo, "rep", scatter_dimension=1, tiled=True).astype(
        jnp.float32
    ) * (1.0 / replicas)
    new_momentum, new_global = outer_update(delta_share, outer_momentum, global_params)
    global_bf = lax.all_gather(new_global.astype(jnp.bfloat16), "rep", axis=1, tiled=True).astype(
        jnp.float32
    )
    master = inner_params[0].astype(jnp.float32)
    stepped = master - 0.8 * (clipped + 0.2 * master)
    merged_params = (0.5 * stepped + 0.5 * global_bf).astype(jnp.bfloat16)
    return (merged_params[None], new_global, new_momentum)


def solution(mesh):
    in_specs = (
        P("rep", "fsdp"),
        P("rep", "fsdp"),
        P("rep", None),
        P("rep", "fsdp", None),
        P("fsdp", "rep"),
        P("fsdp", "rep"),
        P("rep", "fsdp", None),
        P("rep", "fsdp", None),
    )
    out_specs = (P("rep", "fsdp", None), P("fsdp", "rep"), P("fsdp", "rep"))
    return jax.shard_map(
        per_device, mesh=mesh, in_specs=in_specs, out_specs=out_specs, check_vma=False
    )
```

profile of v0, /device:TPU:1, one launch (start us, length us, event | category | flops | bytes accessed | tf_op | source)
XLA Modules:
  0.0 277.3 jit_solution(18043562611079475186)
XLA Ops:
  7.2 0.0 copy-start
  7.2 0.0 reduce-scatter.2.cloned.1.call-start
  7.2 2.4 add_select_fusion.1
  9.6 1.7 fusion.6
  11.3 5.5 %copy.13 = f32[192,1536,2]{0,2,1:T(2,128)} copy(f32[192,1536,2]{1,0,2:T(8,128)} %fusion.6) | data formatting | bytes 4718592 | tf_op jit(solution)/shard_map/convert_element_type | solution.py:19
  16.8 5.3 %convert_element_type.44 = f32[192,3072]{0,1:T(8,128)} reshape(f32[192,1536,2]{0,2,1:T(2,128)} %copy.13) | data formatting | bytes 4718592 | tf_op jit(solution)/shard_map/convert_element_type | solution.py:19
  22.1 0.0 copy-start.4
  22.1 3.4 %copy.15 = f32[192,3072]{1,0:T(8,128)} copy(f32[192,3072]{0,1:T(8,128)} %convert_element_type.44) | data formatting | bytes 4718592 | tf_op jit(solution)/shard_map/convert_element_type | solution.py:19
  25.5 0.0 copy-done.4
  25.5 0.1 copy.14
  25.6 0.0 copy-start.1
  25.6 0.7 mul.83
  26.2 1.0 copy-done.1
  27.2 0.0 copy-start.2
  27.2 0.0 copy-start.3
  27.2 1.5 fusion.5
  28.7 0.0 reduce-scatter.2.cloned.1.call-update
  28.7 0.0 all-gather.2.cloned.1.call-start
  28.8 69.3 %reduce-scatter.2.cloned.1.call-done = bf16[192,256]{1,0:T(8,128)(2,1)} async-done(((bf16[192,3072]{1,0:T(8,128)(2,1)}), bf16[192,256]{1,0:T(8,128)(2,1)}) %reduce-scatter.2.cloned.1.call-update) | async-done | bytes 98320 | tf_op jit(solution)/shard_map/reduce_scatter | solution.py:43
  98.0 0.0 copy-done.2
  98.1 0.0 copy-done.3
  98.1 1.7 fusion.20
  99.8 0.0 all-gather.2.cloned.1.call-update
  99.8 0.0 copy-done
  99.8 3.9 %multiply_reduce_fusion = (f32[]{:T(128)}, f32[192,3072]{1,0:T(8,128)}) fusion(bf16[512,3072]{1,0:T(8,128)(2,1)S(1)} %copy-done, bf16[512,192]{0,1:T(8,128)(2,1)} %param.9, bf16[512,192]{0,1:T(8,128)(2,1)} %param.8), kind=kOutput, calls=%fused_computation.11 | convolution fusion | flops 606535680 | bytes 5898244 | tf_op jit(solution)/shard_map/dot_general | solution.py:36
  103.7 162.0 %psum.7 = f32[]{:T(128)} all-reduce(f32[]{:T(128)} %get-tuple-element.8), channel_id=1, replica_groups=mesh['rep'=12,'fsdp'=64] {'fsdp'}, use_global_device_ids=true, to_apply=%region_1.0 | all-reduce | flops 1 | bytes 8 | tf_op jit(solution)/shard_map/psum | solution.py:39
  266.4 0.0 all-gather.2.cloned.1.call-done
  266.4 4.1 %fusion.7 = bf16[1,192,3072]{2,1,0:T(8,128)(2,1)} fusion(bf16[192,3072]{1,0:T(8,128)(2,1)} %all-gather.2.cloned.1.call-done, f32[192,3072]{1,0:T(8,128)} %get-tuple-element.9, bf16[1,192,3072]{2,1,0:T(8,128)(2,1)} %param.11, f32[]{:T(128)S(6)} %mul.75), kind=kLoop, calls=%fused_computation.17 | loop fusion | flops 5898240 | bytes 5898244 | tf_op jit(solution)/shard_map/broadcast_in_dim | solution.py:53
Async XLA Ops:
  7.2 92.6 %copy-start = (bf16[512,3072]{1,0:T(8,128)(2,1)S(1)}, bf16[512,3072]{1,0:T(8,128)(2,1)}, u32[]{:S(2)}) copy-start(bf16[512,3072]{1,0:T(8,128)(2,1)} %param.10) | copy-start | bytes 9437188
  7.2 90.9 %reduce-scatter.2.cloned.1.call-start = ((), (), s32[]{:S(2)}) async-start(), calls=%async_computation.1 | async-start | bytes 1277952 | tf_op jit(solution)/shard_map/reduce_scatter | solution.py:43
  22.1 3.4 %copy-start.4 = (f32[1,192,24]{1,2,0:T(8,128)S(1)}, f32[1,192,24]{1,2,0:T(8,128)}, u32[]{:S(2)}) copy-start(f32[1,192,24]{1,2,0:T(8,128)} %param.15) | copy-start | bytes 55300
  25.6 1.7 copy-start.1
  27.2 70.8 %copy-start.2 = (f32[192,256]{1,0:T(8,128)S(1)}, f32[192,256]{1,0:T(8,128)}, u32[]{:S(2)}) copy-start(f32[192,256]{1,0:T(8,128)} %param.12) | copy-start | bytes 589828
  27.2 70.8 %copy-start.3 = (f32[192,256]{1,0:T(8,128)S(1)}, f32[192,256]{1,0:T(8,128)}, u32[]{:S(2)}) copy-start(f32[192,256]{1,0:T(8,128)} %param.13) | copy-start | bytes 589828
  28.7 237.7 %all-gather.2.cloned.1.call-start = ((), (), s32[]{:S(2)}) async-start(), calls=%async_computation.2 | async-start | bytes 1277952 | tf_op jit(solution)/shard_map/all_gather | solution.py:47
Sparse Core Ops, SparseCore 0:
  28.9 69.1 reduce-scatter.1
  101.2 67.9 all-gather.1
where the time goes:
time: 278 us; the launch traced here: 277 us
  blocking collectives  162 us (58%)
  waiting for transfers between devices  69.3 us (25%)
  local copies, waits for them, and re-layouts  15.9 us (6%)
  between operations  14.8 us (5%)
  other arithmetic  11.4 us (4%)
  matrix products  3.86 us (1%)
    psum x1, blocking collectives, per_device(): square_total = lax.psum(jnp.sum(grads * grads), 'fsdp')  162 us
    reduce_scatter x1, waiting for transfers between devices, per_device(): lax.psum_scatter(pseudo, 'rep', scatter_dimension=1, tiled=True)  69.3 us
    convert_element_type x3, local copies, waits for them, and re-layouts, unpack(): centered = (unpacked - 8).astype(jnp.float32)  14.1 us
  transfers between devices with their start and end apart: 2, of which 1 were waited for; matrix products, arithmetic and copies ran while one was open for 1% of the time, Pallas kernels for 0%

commit v1 on v0

v1 whole, which is shorter than its diff:
```python
import jax
import jax.numpy as jnp
from jax import lax
from jax.experimental import pallas as pl
from jax.experimental.pallas import tpu as pltpu
from jax.sharding import Mesh, PartitionSpec as P

REP = ("x", "zl")
FSDP = ("zh", "y", "core")
VMEM_BYTES = 32 * 1024 * 1024


def unpack_kernel(words_ref, scales_ref, out_ref):
    scales = scales_ref[...].T
    first = lax.broadcasted_iota(jnp.int32, (words_ref.shape[0], 128), 1) < 64
    for c in range(out_ref.shape[0]):
        words = words_ref[:, c * 128 : (c + 1) * 128]
        scale = jnp.where(first, scales[:, 2 * c : 2 * c + 1], scales[:, 2 * c + 1 : 2 * c + 2])
        low = ((words & 15) - 8).astype(jnp.float32) * scale
        high = ((words >> 4) - 8).astype(jnp.float32) * scale
        out_ref[c, :, :128] = low.astype(jnp.bfloat16)
        out_ref[c, :, 128:] = high.astype(jnp.bfloat16)


def unpack(words, scales_t, parts):
    rows = words.shape[0]
    return pl.pallas_call(
        unpack_kernel,
        out_shape=jax.ShapeDtypeStruct((parts, rows, 256), jnp.bfloat16),
        compiler_params=pltpu.CompilerParams(vmem_limit_bytes=VMEM_BYTES),
        name="unpack",
    )(words, scales_t)


def grads_kernel(gate_ref, up_ref, out_grad_ref, grads_ref, total_ref):
    gate = gate_ref[...].astype(jnp.float32)
    up = up_ref[...].astype(jnp.float32)
    hidden = (gate * jax.nn.sigmoid(gate) * up).astype(jnp.bfloat16)
    tokens = gate_ref.shape[1]
    width = out_grad_ref.shape[1]
    total = jnp.zeros((8, 512), jnp.float32)
    for c in range(0, width, 512):
        part = lax.dot_general(
            hidden,
            out_grad_ref[:, c : c + 512],
            (((1,), (0,)), ((), ())),
            preferred_element_type=jnp.float32,
        ) * (1.0 / tokens)
        grads_ref[:, c : c + 512] = part
        total += jnp.sum((part * part).reshape(-1, 8, 512), axis=0)
    total_ref[...] = jnp.broadcast_to(jnp.sum(total), (8, 128))


def gradients(gate_t, up_t, out_grad):
    rows = gate_t.shape[0]
    width = out_grad.shape[1]
    return pl.pallas_call(
        grads_kernel,
        out_shape=(
            jax.ShapeDtypeStruct((rows, width), jnp.float32),
            jax.ShapeDtypeStruct((8, 128), jnp.float32),
        ),
        compiler_params=pltpu.CompilerParams(vmem_limit_bytes=VMEM_BYTES),
        cost_estimate=pl.CostEstimate(
            flops=2 * rows * width * gate_t.shape[1], bytes_accessed=6_000_000, transcendentals=100_000
        ),
        name="gradients",
    )(gate_t, up_t, out_grad)


def update_kernel(replicas, parts_ref, momentum_ref, params_ref, global_ref, momentum_out_ref, bf_ref):
    row = lax.broadcasted_iota(jnp.int32, (256, 256), 0)
    col = lax.broadcasted_iota(jnp.int32, (256, 256), 1)
    weave = ((row & 127) * 2 + (row >> 7) == col).astype(jnp.bfloat16)
    delta = jnp.zeros(momentum_ref.shape, jnp.float32)
    for c in range(parts_ref.shape[0]):
        delta += jnp.dot(parts_ref[c], weave, preferred_element_type=jnp.float32)
    delta = delta * (1.0 / replicas)
    momentum = 0.9 * momentum_ref[...] + delta
    new_global = params_ref[...] - 0.7 * (delta + 0.9 * momentum)
    momentum_out_ref[...] = momentum
    global_ref[...] = new_global
    bf = new_global.astype(jnp.bfloat16)
    for c in range(bf_ref.shape[0]):
        bf_ref[c] = bf


def update(parts, momentum, params):
    shape = jax.ShapeDtypeStruct(momentum.shape, jnp.float32)
    import functools
    return pl.pallas_call(
        functools.partial(update_kernel, parts.shape[0]),
        out_shape=(shape, shape, jax.ShapeDtypeStruct(parts.shape, jnp.bfloat16)),
        compiler_params=pltpu.CompilerParams(vmem_limit_bytes=VMEM_BYTES),
        name="update",
    )(parts, momentum, params)


def merge_kernel(total_ref, grads_ref, inner_ref, global_ref, out_ref):
    entries = 12288 * 3072
    root_mean = jnp.sqrt(total_ref[:1, :1] / entries + 1e-6)
    clip = jnp.minimum(1.0, 0.02 / root_mean)
    for c in range(global_ref.shape[0]):
        cols = slice(c * 256, (c + 1) * 256)
        clipped = grads_ref[:, cols] * clip
        master = inner_ref[:, cols].astype(jnp.float32)
        stepped = master - 0.8 * (clipped + 0.2 * master)
        out_ref[:, cols] = (0.5 * stepped + 0.5 * global_ref[c].astype(jnp.float32)).astype(jnp.bfloat16)


def merge(total, grads, inner, global_parts):
    return pl.pallas_call(
        merge_kernel,
        out_shape=jax.ShapeDtypeStruct(inner.shape, jnp.bfloat16),
        compiler_params=pltpu.CompilerParams(vmem_limit_bytes=VMEM_BYTES),
        name="merge",
    )(total, grads, inner, global_parts)


def per_device(gate_pre, up_pre, out_grad, inner_params, global_params, outer_momentum, pair_codes, code_scales):
    replicas = lax.axis_size(REP)
    pseudo = unpack(pair_codes[0], code_scales[0].T, replicas)
    parts = lax.all_to_all(pseudo, REP, 0, 0, tiled=True)
    grads, total = gradients(gate_pre.T, up_pre.T, out_grad)
    for axis in ("core", "y", "zh"):
        total = lax.psum(total, axis)
    new_global, new_momentum, global_bf = update(parts, outer_momentum, global_params)
    global_parts = lax.all_to_all(global_bf, REP, 0, 0, tiled=True)
    merged = merge(total, grads, inner_params[0], global_parts)
    return (merged[None], new_global, new_momentum)


def solution(mesh):
    fine = Mesh(mesh.devices.reshape(4, 3, 4, 8, 2), REP + FSDP)
    in_specs = (
        P(REP, FSDP),
        P(REP, FSDP),
        P(REP, None),
        P(REP, FSDP, None),
        P(FSDP, REP),
        P(FSDP, REP),
        P(REP, FSDP, None),
        P(REP, FSDP, None),
    )
    out_specs = (P(REP, FSDP, None), P(FSDP, REP), P(FSDP, REP))
    return jax.shard_map(
        per_device, mesh=fine, in_specs=in_specs, out_specs=out_specs, check_vma=False
    )
```

time: 278 us -> 88.3 us (0.32)
  the two profiles are of different devices: /device:TPU:1 before, /device:TPU:2 now
where the time goes in v1:
time: 88.3 us; the launch traced here: 87.8 us
  blocking collectives  69.6 us (79%)
  local copies, waits for them, and re-layouts  7.02 us (8%)
  Pallas kernels  5.51 us (6%)
  starting transfers between devices  5.03 us (6%)
    psum x3, blocking collectives, per_device(): total = lax.psum(total, axis)  40.5 us
    all_to_all x1, blocking collectives, per_device(): parts = lax.all_to_all(pseudo, REP, 0, 0, tiled=True)  29.1 us
    unnamed x16, local copies, waits for them, and re-layouts  7.02 us
    all_to_all x1, starting transfers between devices, per_device(): global_parts = lax.all_to_all(global_bf, REP, 0, 0, tiled=True)  5.03 us
    pallas_call x1, Pallas kernels, merge(): pl.pallas_call(merge_kernel, out_shape=jax.ShapeDtypeStruct(inner.shape,...  2.09 us
  transfers between devices with their start and end apart: 1, of which 0 were waited for; matrix products, arithmetic and copies ran while one was open for 0% of the time, Pallas kernels for 1%

profile of v1, /device:TPU:2, one launch (start us, length us, event | category | flops | bytes accessed | tf_op | source)
XLA Modules:
  0.0 87.8 jit_solution(16586648794871902448)
XLA Ops:
  0.6 0.0 copy-start.2
  0.6 1.3 %copy-done.2 = s32[1,192,1536]{2,1,0:T(8,128)S(1)} copy-done((s32[1,192,1536]{2,1,0:T(8,128)S(1)}, s32[1,192,1536]{2,1,0:T(8,128)}, u32[]{:S(2)}) %copy-start.2) | copy-done | bytes 1179672
  1.9 0.0 copy-start.7
  1.9 0.7 copy-done.7
  2.6 0.8 unpack.1
  3.4 0.0 copy-start.3
  3.4 0.0 copy-start.4
  3.5 29.1 %all_to_all.10.parts_ref = bf16[12,192,256]{2,1,0:T(8,128)(2,1)S(1)} all-to-all(bf16[12,192,256]{2,1,0:T(8,128)(2,1)S(1)} %unpack.1), channel_id=1, replica_groups=mesh['x'=4,'zl'=3,'zh'=4,'y'=8,'core'=2] {'x','zl'}, dimensions={0} | all-to-all | bytes 2359296 | tf_op jit(solution)/shard_map/all_to_all | solution.py:123
  32.5 0.0 copy-done.3
  32.5 0.0 copy-done.4
  32.5 1.7 %update.1 = (f32[192,256]{1,0:T(8,128)}, f32[192,256]{1,0:T(8,128)}, bf16[12,192,256]{2,1,0:T(8,128)(2,1)}) custom-call(bf16[12,192,256]{2,1,0:T(8,128)(2,1)S(1)} %all_to_all.10.parts_ref, f32[192,256]{1,0:T(8,128)S(1)} %copy-done.3, f32[192,256]{1,0:T(8,128)S(1)} %copy-done.4), custom_call_target="tpu_custom_call" | custom-call | tf_op jit(solution)/shard_map/update/pallas_call | solution.py:91
  34.3 5.0 %all-to-all-start.1 = ((bf16[12,192,256]{2,1,0:T(8,128)(2,1)}), bf16[12,192,256]{2,1,0:T(8,128)(2,1)S(1)}, u32[]{:S(2)}, u32[]{:S(2)}) async-start(bf16[12,192,256]{2,1,0:T(8,128)(2,1)} %get-tuple-element.10), calls=%async_computation.1 | async-start | bytes 2359296 | tf_op jit(solution)/shard_map/all_to_all | solution.py:128
  39.3 0.0 copy-start
  39.3 1.9 %copy-done = bf16[512,3072]{1,0:T(8,128)(2,1)S(1)} copy-done((bf16[512,3072]{1,0:T(8,128)(2,1)S(1)}, bf16[512,3072]{1,0:T(8,128)(2,1)}, u32[]{:S(2)}) %copy-start) | copy-done | bytes 3145752
  41.2 0.0 copy-start.5
  41.2 0.9 %copy-done.5 = bf16[512,192]{0,1:T(8,128)(2,1)S(1)} copy-done((bf16[512,192]{0,1:T(8,128)(2,1)S(1)}, bf16[512,192]{0,1:T(8,128)(2,1)}, u32[]{:S(2)}) %copy-start.5) | copy-done | bytes 196632
  42.1 0.0 copy-start.6
  42.1 0.9 %copy-done.6 = bf16[512,192]{0,1:T(8,128)(2,1)S(1)} copy-done((bf16[512,192]{0,1:T(8,128)(2,1)S(1)}, bf16[512,192]{0,1:T(8,128)(2,1)}, u32[]{:S(2)}) %copy-start.6) | copy-done | bytes 196632
  43.0 0.9 %gradients.1 = (f32[192,3072]{1,0:T(8,128)S(1)}, f32[8,128]{1,0:T(8,128)S(1)}) custom-call(bf16[192,512]{1,0:T(8,128)(2,1)S(1)} %bitcast.10, bf16[192,512]{1,0:T(8,128)(2,1)S(1)} %bitcast.11, bf16[512,3072]{1,0:T(8,128)(2,1)S(1)} %copy-done), custom_call_target="tpu_custom_call" | custom-call | flops 603979776 | bytes 6000000 | tf_op jit(solution)/shard_map/gradients/pallas_call | solution.py:57
  44.0 2.5 %psum.21 = f32[8,128]{1,0:T(8,128)S(1)} all-reduce(f32[8,128]{1,0:T(8,128)S(1)} %get-tuple-element.8), channel_id=1, replica_groups=mesh['x'=4,'zl'=3,'zh'=4,'y'=8,'core'=2] {'core'}, use_global_device_ids=true, to_apply=%region_0.0 | all-reduce | flops 1024 | bytes 8192 | tf_op jit(solution)/shard_map/psum | solution.py:126
  46.4 17.6 %psum.22 = f32[8,128]{1,0:T(8,128)S(1)} all-reduce(f32[8,128]{1,0:T(8,128)S(1)} %psum.21), channel_id=1, replica_groups=mesh['x'=4,'zl'=3,'zh'=4,'y'=8,'core'=2] {'y'}, use_global_device_ids=true, to_apply=%region_1.0 | all-reduce | flops 1024 | bytes 8192 | tf_op jit(solution)/shard_map/psum | solution.py:126
  64.0 20.4 %psum.23.total_ref = f32[8,128]{1,0:T(8,128)S(1)} all-reduce(f32[8,128]{1,0:T(8,128)S(1)} %psum.22), channel_id=1, replica_groups=mesh['x'=4,'zl'=3,'zh'=4,'y'=8,'core'=2] {'zh'}, use_global_device_ids=true, to_apply=%region_2.0 | all-reduce | flops 1024 | bytes 8192 | tf_op jit(solution)/shard_map/psum | solution.py:126
  84.4 0.0 all-to-all-done.1.global_ref
  84.4 0.0 copy-start.1
  84.4 1.3 %copy-done.1 = bf16[1,192,3072]{2,1,0:T(8,128)(2,1)S(1)} copy-done((bf16[1,192,3072]{2,1,0:T(8,128)(2,1)S(1)}, bf16[1,192,3072]{2,1,0:T(8,128)(2,1)}, u32[]{:S(2)}) %copy-start.1) | copy-done | bytes 1179672
  85.7 2.1 %merge.1 = bf16[192,3072]{1,0:T(8,128)(2,1)} custom-call(f32[8,128]{1,0:T(8,128)S(1)} %psum.23.total_ref, f32[192,3072]{1,0:T(8,128)S(1)} %get-tuple-element.9.grads_ref, bf16[192,3072]{1,0:T(8,128)(2,1)S(1)} %bitcast.8, bf16[12,192,256]{2,1,0:T(8,128)(2,1)S(1)} %all-to-all-done.1.global_ref), custom_call_target="tpu_custom_call" | custom-call | tf_op jit(solution)/shard_map/merge/pallas_call | solution.py:112
Async XLA Ops:
  0.6 1.3 %copy-start.2 = (s32[1,192,1536]{2,1,0:T(8,128)S(1)}, s32[1,192,1536]{2,1,0:T(8,128)}, u32[]{:S(2)}) copy-start(s32[1,192,1536]{2,1,0:T(8,128)} %param.14) | copy-start | bytes 3538948
  1.9 0.7 copy-start.7
  3.4 29.1 %copy-start.3 = (f32[192,256]{1,0:T(8,128)S(1)}, f32[192,256]{1,0:T(8,128)}, u32[]{:S(2)}) copy-start(f32[192,256]{1,0:T(8,128)} %momentum_ref.1) | copy-start | bytes 589828
  3.4 29.1 %copy-start.4 = (f32[192,256]{1,0:T(8,128)S(1)}, f32[192,256]{1,0:T(8,128)}, u32[]{:S(2)}) copy-start(f32[192,256]{1,0:T(8,128)} %params_ref.1) | copy-start | bytes 589828
  34.3 50.2 %all-to-all-start.1 = ((bf16[12,192,256]{2,1,0:T(8,128)(2,1)}), bf16[12,192,256]{2,1,0:T(8,128)(2,1)S(1)}, u32[]{:S(2)}, u32[]{:S(2)}) async-start(bf16[12,192,256]{2,1,0:T(8,128)(2,1)} %get-tuple-element.10), calls=%async_computation.1 | async-start | bytes 2359296 | tf_op jit(solution)/shard_map/all_to_all | solution.py:128
  39.3 1.9 %copy-start = (bf16[512,3072]{1,0:T(8,128)(2,1)S(1)}, bf16[512,3072]{1,0:T(8,128)(2,1)}, u32[]{:S(2)}) copy-start(bf16[512,3072]{1,0:T(8,128)(2,1)} %out_grad_ref.1) | copy-start | bytes 9437188
  41.2 0.9 %copy-start.5 = (bf16[512,192]{0,1:T(8,128)(2,1)S(1)}, bf16[512,192]{0,1:T(8,128)(2,1)}, u32[]{:S(2)}) copy-start(bf16[512,192]{0,1:T(8,128)(2,1)} %param.8) | copy-start | bytes 589828
  42.1 0.9 %copy-start.6 = (bf16[512,192]{0,1:T(8,128)(2,1)S(1)}, bf16[512,192]{0,1:T(8,128)(2,1)}, u32[]{:S(2)}) copy-start(bf16[512,192]{0,1:T(8,128)(2,1)} %param.9) | copy-start | bytes 589828
  84.4 1.3 %copy-start.1 = (bf16[1,192,3072]{2,1,0:T(8,128)(2,1)S(1)}, bf16[1,192,3072]{2,1,0:T(8,128)(2,1)}, u32[]{:S(2)}) copy-start(bf16[1,192,3072]{2,1,0:T(8,128)(2,1)} %param.11) | copy-start | bytes 3538948

commit v2 on v1

v2 whole, which is shorter than its diff:
```python
import jax
import jax.numpy as jnp
from jax import lax
from jax.experimental import pallas as pl
from jax.experimental.pallas import tpu as pltpu
from jax.sharding import Mesh, PartitionSpec as P

REP = ("x", "zl")
FSDP = ("zh", "y", "core")
REPLICAS = 12
ENTRIES = 12288 * 3072
MIB = 1024 * 1024
ANY = pl.BlockSpec(memory_space=pl.ANY)


def hbm(x):
    return pltpu.with_memory_space_constraint(x, pltpu.HBM)


def unpack_kernel(words_hbm, scales_hbm, out_hbm, order_ref, words_ref, scales_ref, out_ref, sems):
    steps, per_step, rows, _ = out_ref.shape
    span = per_step * 128
    copies_in = [pltpu.make_async_copy(scales_hbm, scales_ref, sems.at[0])]
    for i in range(steps):
        cols = pl.ds(i * span, span)
        copies_in.append(
            pltpu.make_async_copy(words_hbm.at[:, cols], words_ref.at[:, cols], sems.at[1 + i])
        )
    for copy in copies_in:
        copy.start()
    order_ref[...] = jnp.zeros(order_ref.shape, jnp.float32)
    first = lax.broadcasted_iota(jnp.int32, (rows, 128), 1) < 64
    copies_in[0].wait()
    scales = scales_ref[...].T
    copies_out = []
    for i in range(steps):
        copies_in[1 + i].wait()
        for k in range(per_step):
            c = i * per_step + k
            words = words_ref[:, c * 128 : (c + 1) * 128]
            scale = jnp.where(first, scales[:, 2 * c : 2 * c + 1], scales[:, 2 * c + 1 : 2 * c + 2])
            low = ((words & 15) - 8).astype(jnp.float32) * scale
            high = ((words >> 4) - 8).astype(jnp.float32) * scale
            out_ref[i, k, :, :128] = low.astype(jnp.bfloat16)
            out_ref[i, k, :, 128:] = high.astype(jnp.bfloat16)
        copies_out.append(pltpu.make_async_copy(out_ref.at[i], out_hbm.at[i], sems.at[1 + steps + i]))
        copies_out[-1].start()
    for copy in copies_out:
        copy.wait()


def unpack(words, scales_t):
    rows, width = words.shape
    shape = (4, REPLICAS // 4, rows, 256)
    return pl.pallas_call(
        unpack_kernel,
        in_specs=[ANY, ANY],
        out_specs=(ANY, pl.BlockSpec(memory_space=pltpu.VMEM)),
        out_shape=(
            pltpu.HBM(shape, jnp.bfloat16),
            pltpu.VMEM((8, 128), jnp.float32),
        ),
        scratch_shapes=[
            pltpu.VMEM((rows, width), jnp.int32),
            pltpu.VMEM(scales_t.shape, jnp.float32),
            pltpu.VMEM(shape, jnp.bfloat16),
            pltpu.SemaphoreType.DMA((9,)),
        ],
        compiler_params=pltpu.CompilerParams(vmem_limit_bytes=32 * MIB),
        name="unpack",
    )(hbm(words), hbm(scales_t))


def gradients_kernel(
    order_ref, gate_hbm, up_hbm, out_grad_hbm, momentum_hbm, params_hbm,
    grads_ref, total_ref, momentum_ref, params_ref,
    gate_ref, up_ref, out_grad_ref, sems,
):
    width = out_grad_ref.shape[1]
    steps = width // 512
    columns = [pl.ds(c * 512, 512) for c in range(steps)]
    first = [
        pltpu.make_async_copy(gate_hbm, gate_ref, sems.at[0]),
        pltpu.make_async_copy(up_hbm, up_ref, sems.at[1]),
    ]
    blocks = [
        pltpu.make_async_copy(out_grad_hbm.at[:, cols], out_grad_ref.at[:, cols], sems.at[2 + c])
        for c, cols in enumerate(columns)
    ]
    last = [
        pltpu.make_async_copy(momentum_hbm, momentum_ref, sems.at[2 + steps]),
        pltpu.make_async_copy(params_hbm, params_ref, sems.at[3 + steps]),
    ]
    for copy in first + blocks + last:
        copy.start()
    for copy in first:
        copy.wait()
    gate = gate_ref[...].astype(jnp.float32)
    up = up_ref[...].astype(jnp.float32)
    hidden = (gate * jax.nn.sigmoid(gate) * up).astype(jnp.bfloat16)
    tokens = gate_ref.shape[1]
    total = jnp.zeros((8, 512), jnp.float32)
    for copy, cols in zip(blocks, columns):
        copy.wait()
        part = lax.dot_general(
            hidden, out_grad_ref[:, cols], (((1,), (0,)), ((), ())), preferred_element_type=jnp.float32
        ) * (1.0 / tokens)
        grads_ref[:, cols] = part.astype(jnp.bfloat16)
        total += jnp.sum((part * part).reshape(-1, 8, 512), axis=0)
    total_ref[...] = jnp.broadcast_to(jnp.sum(total), (8, 128)) + order_ref[...]
    for copy in last:
        copy.wait()


def gradients(order, gate_t, up_t, out_grad, momentum, params):
    rows, tokens = gate_t.shape
    width = out_grad.shape[1]
    state = pltpu.VMEM(momentum.shape, jnp.float32)
    return pl.pallas_call(
        gradients_kernel,
        in_specs=[pl.BlockSpec(memory_space=pltpu.VMEM)] + [ANY] * 5,
        out_shape=(
            pltpu.VMEM((rows, width), jnp.bfloat16),
            pltpu.VMEM((8, 128), jnp.float32),
            state,
            state,
        ),
        scratch_shapes=[
            pltpu.VMEM((rows, tokens), jnp.bfloat16),
            pltpu.VMEM((rows, tokens), jnp.bfloat16),
            pltpu.VMEM((tokens, width), jnp.bfloat16),
            pltpu.SemaphoreType.DMA((width // 512 + 4,)),
        ],
        compiler_params=pltpu.CompilerParams(vmem_limit_bytes=32 * MIB),
        cost_estimate=pl.CostEstimate(
            flops=2 * rows * width * tokens, bytes_accessed=6_000_000, transcendentals=rows * tokens
        ),
        name="gradients",
    )(order, *map(hbm, (gate_t, up_t, out_grad, momentum, params)))


def update_kernel(parts_ref, momentum_ref, params_ref, total_ref, bf_hbm, delta_ref, total_out_ref, bf_ref, sems):
    row = lax.broadcasted_iota(jnp.int32, (256, 256), 0)
    col = lax.broadcasted_iota(jnp.int32, (256, 256), 1)
    weave = ((row & 127) * 2 + (row >> 7) == col).astype(jnp.bfloat16)
    delta = jnp.zeros(momentum_ref.shape, jnp.float32)
    for c in range(parts_ref.shape[0]):
        delta += jnp.dot(parts_ref[c], weave, preferred_element_type=jnp.float32)
    delta = delta * (1.0 / REPLICAS)
    momentum = 0.9 * momentum_ref[...] + delta
    new_global = params_ref[...] - 0.7 * (delta + 0.9 * momentum)
    bf_ref[...] = new_global.astype(jnp.bfloat16)
    copies = [pltpu.make_async_copy(bf_ref, bf_hbm.at[c], sems.at[c]) for c in range(bf_hbm.shape[0])]
    for copy in copies:
        copy.start()
    delta_ref[...] = delta
    total_out_ref[...] = total_ref[...]
    for copy in copies:
        copy.wait()


def update(parts, momentum, params, total):
    rows, width = momentum.shape
    vmem = pl.BlockSpec(memory_space=pltpu.VMEM)
    return pl.pallas_call(
        update_kernel,
        out_specs=(ANY, vmem, vmem),
        out_shape=(
            pltpu.HBM((3, rows, width), jnp.bfloat16),
            pltpu.HBM((rows, width), jnp.float32),
            pltpu.VMEM((8, 128), jnp.float32),
        ),
        scratch_shapes=[pltpu.VMEM((rows, width), jnp.bfloat16), pltpu.SemaphoreType.DMA((3,))],
        compiler_params=pltpu.CompilerParams(vmem_limit_bytes=32 * MIB),
        name="update",
    )(parts, momentum, params, total)


def repeat_kernel(block_ref, total_ref, out_hbm, total_out_ref, sems):
    copies = [pltpu.make_async_copy(block_ref, out_hbm.at[i], sems.at[i]) for i in range(out_hbm.shape[0])]
    for copy in copies:
        copy.start()
    total_out_ref[...] = total_ref[...]
    for copy in copies:
        copy.wait()


def repeat(block, total):
    vmem = pl.BlockSpec(memory_space=pltpu.VMEM)
    return pl.pallas_call(
        repeat_kernel,
        out_specs=(ANY, vmem),
        out_shape=(
            pltpu.HBM((4,) + block.shape, block.dtype),
            pltpu.VMEM((8, 128), jnp.float32),
        ),
        scratch_shapes=[pltpu.SemaphoreType.DMA((4,))],
        compiler_params=pltpu.CompilerParams(vmem_limit_bytes=32 * MIB),
        name="repeat",
    )(block, total)


def state_kernel(total_ref, delta_hbm, momentum_hbm, params_hbm, inner_hbm,
                 global_ref, momentum_out_ref, inner_ref, total_out_ref,
                 delta_ref, momentum_ref, params_ref, sems):
    pairs = [
        (delta_hbm, delta_ref), (momentum_hbm, momentum_ref), (params_hbm, params_ref), (inner_hbm, inner_ref)
    ]
    copies = [pltpu.make_async_copy(src, dst, sems.at[i]) for i, (src, dst) in enumerate(pairs)]
    for copy in copies:
        copy.start()
    total_out_ref[...] = total_ref[...]
    for copy in copies[:3]:
        copy.wait()
    momentum = 0.9 * momentum_ref[...] + delta_ref[...]
    momentum_out_ref[...] = momentum
    global_ref[...] = params_ref[...] - 0.7 * (delta_ref[...] + 0.9 * momentum)
    copies[3].wait()


def state(delta, momentum, params, total, inner):
    shape = jax.ShapeDtypeStruct(momentum.shape, jnp.float32)
    block = pltpu.VMEM(momentum.shape, jnp.float32)
    return pl.pallas_call(
        state_kernel,
        in_specs=[pl.BlockSpec(memory_space=pltpu.VMEM)] + [ANY] * 4,
        out_shape=(
            shape,
            shape,
            pltpu.VMEM(inner.shape, inner.dtype),
            pltpu.VMEM((8, 128), jnp.float32),
        ),
        scratch_shapes=[block, block, block, pltpu.SemaphoreType.DMA((4,))],
        compiler_params=pltpu.CompilerParams(vmem_limit_bytes=32 * MIB),
        name="state",
    )(total, *map(hbm, (delta, momentum, params, inner)))


def merge_kernel(total_ref, grads_ref, inner_ref, global_ref, out_hbm, out_ref, sems):
    root_mean = jnp.sqrt(total_ref[:1, :1] / ENTRIES + 1e-6)
    clip = jnp.minimum(1.0, 0.02 / root_mean)
    copies = []
    for c in range(REPLICAS):
        cols = pl.ds(c * 256, 256)
        clipped = grads_ref[:, cols].astype(jnp.float32) * clip
        master = inner_ref[:, cols].astype(jnp.float32)
        stepped = master - 0.8 * (clipped + 0.2 * master)
        mean = 0.5 * stepped + 0.5 * global_ref[c].astype(jnp.float32)
        out_ref[:, cols] = mean.astype(jnp.bfloat16)
        if c % 3 == 2:
            cols = pl.ds((c - 2) * 256, 768)
            copies.append(pltpu.make_async_copy(out_ref.at[:, cols], out_hbm.at[:, cols], sems.at[c // 3]))
            copies[-1].start()
    for copy in copies:
        copy.wait()


def merge(total, grads, inner, global_parts):
    return pl.pallas_call(
        merge_kernel,
        out_specs=ANY,
        out_shape=jax.ShapeDtypeStruct(inner.shape, jnp.bfloat16),
        scratch_shapes=[pltpu.VMEM(inner.shape, jnp.bfloat16), pltpu.SemaphoreType.DMA((4,))],
        compiler_params=pltpu.CompilerParams(vmem_limit_bytes=32 * MIB),
        name="merge",
    )(total, grads, inner, global_parts)


def per_device(gate_pre, up_pre, out_grad, inner_params, global_params, outer_momentum, pair_codes, code_scales):
    pseudo, order = unpack(pair_codes[0], code_scales[0].T)
    grads, total, momentum, params = gradients(order, gate_pre.T, up_pre.T, out_grad, outer_momentum, global_params)
    parts = lax.all_to_all(pseudo.reshape((REPLICAS,) + pseudo.shape[2:]), REP, 0, 0, tiled=True)
    total = lax.psum(total, "y")
    global_bf, delta, total = update(parts, momentum, params, total)
    run_parts = lax.all_to_all(global_bf, "zl", 0, 0, tiled=True)
    total = lax.psum(total, "core")
    new_global, new_momentum, inner, total = state(delta, outer_momentum, global_params, total, inner_params[0])
    run_parts, total = repeat(run_parts, total)
    global_parts = lax.all_to_all(run_parts, "x", 0, 0, tiled=True)
    total = lax.psum(total, "zh")
    merged = merge(total, grads, inner, global_parts.reshape((REPLICAS,) + global_parts.shape[2:]))
    return (merged[None], new_global, new_momentum)


def solution(mesh):
    fine = Mesh(mesh.devices.reshape(4, 3, 4, 8, 2), REP + FSDP)
    in_specs = (
        P(REP, FSDP),
        P(REP, FSDP),
        P(REP, None),
        P(REP, FSDP, None),
        P(FSDP, REP),
        P(FSDP, REP),
        P(REP, FSDP, None),
        P(REP, FSDP, None),
    )
    out_specs = (P(REP, FSDP, None), P(FSDP, REP), P(FSDP, REP))
    return jax.shard_map(
        per_device, mesh=fine, in_specs=in_specs, out_specs=out_specs, check_vma=False
    )
```

time: 88.3 us -> 72.5 us (0.82)
  blocking collectives: 69.6 us -> 35.8 us
  starting transfers between devices: 5.03 us -> 21.6 us
  Pallas kernels: 5.51 us -> 13 us
  local copies, waits for them, and re-layouts: 7.02 us -> 0 us
  waiting for transfers between devices: 0.01 us -> 1.07 us
    all_to_all x1 -> x0, blocking collectives: 29.1 us -> none  [per_device(): parts = lax.all_to_all(pseudo, REP, 0, 0, tiled=True)]
    all_to_all x1 -> x3, starting transfers between devices: 5.03 us -> 21.6 us  [the longest x1 13.1 us: per_device(): lax.all_to_all(pseudo.reshape((REPLICAS,) + pseudo.shape[2:]), REP, 0, 0,...]
    pallas_call x4 -> x6, Pallas kernels: 5.51 us -> 13 us  [the longest x1 3.1 us: gradients(): pl.pallas_call(gradients_kernel, in_specs=[pl.BlockSpec(memory_space=pltp...]
    unnamed x16 -> x0, local copies, waits for them, and re-layouts: 7.02 us -> none
    psum x3, blocking collectives: 40.5 us -> 35.8 us  [the longest x1 19.1 us: per_device(): total = lax.psum(total, 'zh')]
    all_to_all x1 -> x3, waiting for transfers between devices: 0.01 us -> 1.07 us  [the longest x1 1.07 us: per_device(): run_parts = lax.all_to_all(global_bf, 'zl', 0, 0, tiled=True)]
  transfers between devices with their start and end apart: 1 -> 3, of which waited for: 0 -> 1; matrix products, arithmetic and copies ran while one was open for 0% -> 0% of each run, Pallas kernels for 1% -> 8%
where the time goes in v2:
time: 72.5 us; the launch traced here: 72.1 us
  blocking collectives  35.8 us (49%)
  starting transfers between devices  21.6 us (30%)
  Pallas kernels  13 us (18%)
  waiting for transfers between devices  1.07 us (1%)
    psum x1, blocking collectives, per_device(): total = lax.psum(total, 'zh')  19.1 us
    psum x1, blocking collectives, per_device(): total = lax.psum(total, 'y')  14.2 us
    all_to_all x1, starting transfers between devices, per_device(): lax.all_to_all(pseudo.reshape((REPLICAS,) + pseudo.shape[2:]), REP, 0, 0,...  13.1 us
    all_to_all x1, starting transfers between devices, per_device(): global_parts = lax.all_to_all(run_parts, 'x', 0, 0, tiled=True)  4.83 us
    all_to_all x1, starting transfers between devices, per_device(): run_parts = lax.all_to_all(global_bf, 'zl', 0, 0, tiled=True)  3.65 us
    pallas_call x1, Pallas kernels, gradients(): pl.pallas_call(gradients_kernel, in_specs=[pl.BlockSpec(memory_space=pltp...  3.1 us
    pallas_call x1, Pallas kernels, unpack(): pl.pallas_call(unpack_kernel, in_specs=[ANY, ANY], out_specs=(ANY, pl.Blo...  2.69 us
    psum x1, blocking collectives, per_device(): total = lax.psum(total, 'core')  2.45 us
  transfers between devices with their start and end apart: 3, of which 1 were waited for; matrix products, arithmetic and copies ran while one was open for 0% of the time, Pallas kernels for 8%

profile of v2, /device:TPU:2, one launch (start us, length us, event | category | flops | bytes accessed | tf_op | source)
XLA Modules:
  0.0 72.1 jit_solution(2447833061876578874)
XLA Ops:
  0.6 2.7 %unpack.1 = (bf16[4,3,192,256]{3,2,1,0:T(8,128)(2,1)}, f32[8,128]{1,0:T(8,128)S(1)}) custom-call(s32[192,1536]{1,0:T(8,128)} %bitcast.11, f32[24,192]{1,0:T(8,128)} %bitcast.17), custom_call_target="tpu_custom_call" | custom-call | tf_op jit(solution)/shard_map/unpack/pallas_call | solution.py:55
  3.3 13.1 %all-to-all-start = ((bf16[12,192,256]{2,1,0:T(8,128)(2,1)}), bf16[12,192,256]{2,1,0:T(8,128)(2,1)S(1)}, u32[]{:S(2)}, u32[]{:S(2)}) async-start(bf16[12,192,256]{2,1,0:T(8,128)(2,1)} %bitcast.13), calls=%async_computation | async-start | bytes 2359296 | tf_op jit(solution)/shard_map/all_to_all | solution.py:272
  16.4 3.1 %gradients.1 = (bf16[192,3072]{1,0:T(8,128)(2,1)S(1)}, f32[8,128]{1,0:T(8,128)S(1)}, f32[192,256]{1,0:T(8,128)S(1)}, f32[192,256]{1,0:T(8,128)S(1)}) custom-call(f32[8,128]{1,0:T(8,128)S(1)} %get-tuple-element.19.order_ref, bf16[192,512]{1,0:T(8,128)(2,1)} %bitcast.15, bf16[192,512]{1,0:T(8,128)(2,1)} %bitcast.16, bf16[512,3072]{1,0:T(8,128)(2,1)} %out_grad_hbm.1, ...), custom_call_target="tpu_custom_call" | custom-call | flops 603979776 | bytes 6000000 | tf_op jit(solution)/shard_map/gradients/pallas_call | solution.py:119
  19.6 14.2 %psum.21.total_ref = f32[8,128]{1,0:T(8,128)S(1)} all-reduce(f32[8,128]{1,0:T(8,128)S(1)} %get-tuple-element.22), channel_id=1, replica_groups=mesh['x'=4,'zl'=3,'zh'=4,'y'=8,'core'=2] {'y'}, use_global_device_ids=true, to_apply=%region_0.0 | all-reduce | flops 1024 | bytes 8192 | tf_op jit(solution)/shard_map/psum | solution.py:273
  33.7 0.0 all-to-all-done.parts_ref
  33.7 1.9 %update.1 = (bf16[3,192,256]{2,1,0:T(8,128)(2,1)}, f32[192,256]{1,0:T(8,128)}, f32[8,128]{1,0:T(8,128)S(1)}) custom-call(bf16[12,192,256]{2,1,0:T(8,128)(2,1)S(1)} %all-to-all-done.parts_ref, f32[192,256]{1,0:T(8,128)S(1)} %get-tuple-element.20.momentum_ref, f32[192,256]{1,0:T(8,128)S(1)} %get-tuple-element.21.params_ref, f32[8,128]{1,0:T(8,128)S(1)} %psum.21.total_ref), custom_call_target="tpu_custom_call" | custom-call | tf_op jit(solution)/shard_map/update/pallas_call | solution.py:165
  35.6 3.7 %all-to-all-start.1 = ((bf16[3,192,256]{2,1,0:T(8,128)(2,1)}), bf16[3,192,256]{2,1,0:T(8,128)(2,1)S(1)}, u32[]{:S(2)}, u32[]{:S(2)}) async-start(bf16[3,192,256]{2,1,0:T(8,128)(2,1)} %get-tuple-element.23), calls=%async_computation.1 | async-start | bytes 589824 | tf_op jit(solution)/shard_map/all_to_all | solution.py:275
  39.3 2.4 %psum.22.total_ref = f32[8,128]{1,0:T(8,128)S(1)} all-reduce(f32[8,128]{1,0:T(8,128)S(1)} %get-tuple-element.24), channel_id=1, replica_groups=mesh['x'=4,'zl'=3,'zh'=4,'y'=8,'core'=2] {'core'}, use_global_device_ids=true, to_apply=%region_1.0 | all-reduce | flops 1024 | bytes 8192 | tf_op jit(solution)/shard_map/psum | solution.py:276
  41.7 2.4 %state.1 = (f32[192,256]{1,0:T(8,128)}, f32[192,256]{1,0:T(8,128)}, bf16[192,3072]{1,0:T(8,128)(2,1)S(1)}, f32[8,128]{1,0:T(8,128)S(1)}) custom-call(f32[8,128]{1,0:T(8,128)S(1)} %psum.22.total_ref, f32[192,256]{1,0:T(8,128)} %get-tuple-element.25.delta_hbm, f32[192,256]{1,0:T(8,128)} %momentum_hbm.3, f32[192,256]{1,0:T(8,128)} %params_hbm.3, ...), custom_call_target="tpu_custom_call" | custom-call | tf_op jit(solution)/shard_map/state/pallas_call | solution.py:224
  44.1 1.1 %all-to-all-done.1.block_ref = bf16[3,192,256]{2,1,0:T(8,128)(2,1)S(1)} async-done(((bf16[3,192,256]{2,1,0:T(8,128)(2,1)}), bf16[3,192,256]{2,1,0:T(8,128)(2,1)S(1)}, u32[]{:S(2)}, u32[]{:S(2)}) %all-to-all-start.1) | async-done | bytes 294944 | tf_op jit(solution)/shard_map/all_to_all | solution.py:275
  45.2 1.0 %repeat.1 = (bf16[4,3,192,256]{3,2,1,0:T(8,128)(2,1)}, f32[8,128]{1,0:T(8,128)S(1)}) custom-call(bf16[3,192,256]{2,1,0:T(8,128)(2,1)S(1)} %all-to-all-done.1.block_ref, f32[8,128]{1,0:T(8,128)S(1)} %get-tuple-element.26.total_ref), custom_call_target="tpu_custom_call" | custom-call | tf_op jit(solution)/shard_map/repeat/pallas_call | solution.py:190
  46.2 4.8 %all-to-all-start.2 = ((bf16[4,3,192,256]{3,2,1,0:T(8,128)(2,1)}), bf16[4,3,192,256]{3,2,1,0:T(8,128)(2,1)S(1)}, u32[]{:S(2)}, u32[]{:S(2)}) async-start(bf16[4,3,192,256]{3,2,1,0:T(8,128)(2,1)} %get-tuple-element.30), calls=%async_computation.2 | async-start | bytes 2359296 | tf_op jit(solution)/shard_map/all_to_all | solution.py:279
  51.0 19.1 %psum.23.total_ref = f32[8,128]{1,0:T(8,128)S(1)} all-reduce(f32[8,128]{1,0:T(8,128)S(1)} %get-tuple-element.27), channel_id=1, replica_groups=mesh['x'=4,'zl'=3,'zh'=4,'y'=8,'core'=2] {'zh'}, use_global_device_ids=true, to_apply=%region_2.0 | all-reduce | flops 1024 | bytes 8192 | tf_op jit(solution)/shard_map/psum | solution.py:280
  70.2 0.0 all-to-all-done.2
  70.2 1.9 %merge.1 = bf16[192,3072]{1,0:T(8,128)(2,1)} custom-call(f32[8,128]{1,0:T(8,128)S(1)} %psum.23.total_ref, bf16[192,3072]{1,0:T(8,128)(2,1)S(1)} %get-tuple-element.28.grads_ref, bf16[192,3072]{1,0:T(8,128)(2,1)S(1)} %get-tuple-element.29.inner_ref, bf16[12,192,256]{2,1,0:T(8,128)(2,1)S(1)} %bitcast.10), custom_call_target="tpu_custom_call" | custom-call | tf_op jit(solution)/shard_map/merge/pallas_call | solution.py:259
Async XLA Ops:
  3.3 30.4 %all-to-all-start = ((bf16[12,192,256]{2,1,0:T(8,128)(2,1)}), bf16[12,192,256]{2,1,0:T(8,128)(2,1)S(1)}, u32[]{:S(2)}, u32[]{:S(2)}) async-start(bf16[12,192,256]{2,1,0:T(8,128)(2,1)} %bitcast.13), calls=%async_computation | async-start | bytes 2359296 | tf_op jit(solution)/shard_map/all_to_all | solution.py:272
  35.6 9.5 %all-to-all-start.1 = ((bf16[3,192,256]{2,1,0:T(8,128)(2,1)}), bf16[3,192,256]{2,1,0:T(8,128)(2,1)S(1)}, u32[]{:S(2)}, u32[]{:S(2)}) async-start(bf16[3,192,256]{2,1,0:T(8,128)(2,1)} %get-tuple-element.23), calls=%async_computation.1 | async-start | bytes 589824 | tf_op jit(solution)/shard_map/all_to_all | solution.py:275
  46.2 24.0 %all-to-all-start.2 = ((bf16[4,3,192,256]{3,2,1,0:T(8,128)(2,1)}), bf16[4,3,192,256]{3,2,1,0:T(8,128)(2,1)S(1)}, u32[]{:S(2)}, u32[]{:S(2)}) async-start(bf16[4,3,192,256]{3,2,1,0:T(8,128)(2,1)} %get-tuple-element.30), calls=%async_computation.2 | async-start | bytes 2359296 | tf_op jit(solution)/shard_map/all_to_all | solution.py:279

commit v3 on v2

--- a/solution.py
+++ b/solution.py
@@ -115,15 +115,14 @@
 def gradients(order, gate_t, up_t, out_grad, momentum, params):
     rows, tokens = gate_t.shape
     width = out_grad.shape[1]
-    state = pltpu.VMEM(momentum.shape, jnp.float32)
     return pl.pallas_call(
         gradients_kernel,
         in_specs=[pl.BlockSpec(memory_space=pltpu.VMEM)] + [ANY] * 5,
         out_shape=(
             pltpu.VMEM((rows, width), jnp.bfloat16),
             pltpu.VMEM((8, 128), jnp.float32),
-            state,
-            state,
+            pltpu.VMEM(momentum.shape, jnp.float32),
+            pltpu.VMEM(params.shape, jnp.float32),
         ),
         scratch_shapes=[
             pltpu.VMEM((rows, tokens), jnp.bfloat16),
@@ -139,117 +138,84 @@
     )(order, *map(hbm, (gate_t, up_t, out_grad, momentum, params)))
 
 
-def update_kernel(parts_ref, momentum_ref, params_ref, total_ref, bf_hbm, delta_ref, total_out_ref, bf_ref, sems):
+def update_kernel(parts_ref, total_ref, momentum_ref, params_ref,
+                  bf_hbm, global_hbm, momentum_hbm, total_out_ref, momentum_out_ref, global_ref, bf_ref, sems):
     row = lax.broadcasted_iota(jnp.int32, (256, 256), 0)
     col = lax.broadcasted_iota(jnp.int32, (256, 256), 1)
     weave = ((row & 127) * 2 + (row >> 7) == col).astype(jnp.bfloat16)
     delta = jnp.zeros(momentum_ref.shape, jnp.float32)
-    for c in range(parts_ref.shape[0]):
+    for c in range(REPLICAS):
         delta += jnp.dot(parts_ref[c], weave, preferred_element_type=jnp.float32)
     delta = delta * (1.0 / REPLICAS)
     momentum = 0.9 * momentum_ref[...] + delta
     new_global = params_ref[...] - 0.7 * (delta + 0.9 * momentum)
     bf_ref[...] = new_global.astype(jnp.bfloat16)
-    copies = [pltpu.make_async_copy(bf_ref, bf_hbm.at[c], sems.at[c]) for c in range(bf_hbm.shape[0])]
+    copies = [pltpu.make_async_copy(bf_ref, bf_hbm.at[c], sems.at[c]) for c in range(REPLICAS)]
     for copy in copies:
         copy.start()
-    delta_ref[...] = delta
+    momentum_out_ref[...] = momentum
+    global_ref[...] = new_global
+    outs = [
+        pltpu.make_async_copy(momentum_out_ref, momentum_hbm, sems.at[REPLICAS]),
+        pltpu.make_async_copy(global_ref, global_hbm, sems.at[REPLICAS + 1]),
+    ]
+    for copy in outs:
+        copy.start()
     total_out_ref[...] = total_ref[...]
-    for copy in copies:
+    for copy in copies + outs:
         copy.wait()
 
 
 def update(parts, momentum, params, total):
     rows, width = momentum.shape
     vmem = pl.BlockSpec(memory_space=pltpu.VMEM)
+    state = pltpu.HBM((rows, width), jnp.float32)
     return pl.pallas_call(
         update_kernel,
-        out_specs=(ANY, vmem, vmem),
+        out_specs=(ANY, ANY, ANY, vmem),
         out_shape=(
-            pltpu.HBM((3, rows, width), jnp.bfloat16),
-            pltpu.HBM((rows, width), jnp.float32),
-            pltpu.VMEM((8, 128), jnp.float32),
-        ),
-        scratch_shapes=[pltpu.VMEM((rows, width), jnp.bfloat16), pltpu.SemaphoreType.DMA((3,))],
+            pltpu.HBM((REPLICAS, rows, width), jnp.bfloat16), state, state, pltpu.VMEM((8, 128), jnp.float32)
+        ),
+        scratch_shapes=[
+            pltpu.VMEM((rows, width), jnp.float32),
+            pltpu.VMEM((rows, width), jnp.float32),
+            pltpu.VMEM((rows, width), jnp.bfloat16),
+            pltpu.SemaphoreType.DMA((REPLICAS + 2,)),
+        ],
         compiler_params=pltpu.CompilerParams(vmem_limit_bytes=32 * MIB),
         name="update",
-    )(parts, momentum, params, total)
-
-
-def repeat_kernel(block_ref, total_ref, out_hbm, total_out_ref, sems):
-    copies = [pltpu.make_async_copy(block_ref, out_hbm.at[i], sems.at[i]) for i in range(out_hbm.shape[0])]
-    for copy in copies:
-        copy.start()
+    )(parts, total, momentum, params)
+
+
+def stage_kernel(total_ref, inner_hbm, inner_ref, total_out_ref, sem):
+    copy = pltpu.make_async_copy(inner_hbm, inner_ref, sem)
+    copy.start()
     total_out_ref[...] = total_ref[...]
-    for copy in copies:
-        copy.wait()
-
-
-def repeat(block, total):
-    vmem = pl.BlockSpec(memory_space=pltpu.VMEM)
-    return pl.pallas_call(
-        repeat_kernel,
-        out_specs=(ANY, vmem),
-        out_shape=(
-            pltpu.HBM((4,) + block.shape, block.dtype),
-            pltpu.VMEM((8, 128), jnp.float32),
-        ),
-        scratch_shapes=[pltpu.SemaphoreType.DMA((4,))],
-        compiler_params=pltpu.CompilerParams(vmem_limit_bytes=32 * MIB),
-        name="repeat",
-    )(block, total)
-
-
-def state_kernel(total_ref, delta_hbm, momentum_hbm, params_hbm, inner_hbm,
-                 global_ref, momentum_out_ref, inner_ref, total_out_ref,
-                 delta_ref, momentum_ref, params_ref, sems):
-    pairs = [
-        (delta_hbm, delta_ref), (momentum_hbm, momentum_ref), (params_hbm, params_ref), (inner_hbm, inner_ref)
-    ]
-    copies = [pltpu.make_async_copy(src, dst, sems.at[i]) for i, (src, dst) in enumerate(pairs)]
-    for copy in copies:
-        copy.start()
-    total_out_ref[...] = total_ref[...]
-    for copy in copies[:3]:
-        copy.wait()
-    momentum = 0.9 * momentum_ref[...] + delta_ref[...]
-    momentum_out_ref[...] = momentum
-    global_ref[...] = params_ref[...] - 0.7 * (delta_ref[...] + 0.9 * momentum)
-    copies[3].wait()
-
-
-def state(delta, momentum, params, total, inner):
-    shape = jax.ShapeDtypeStruct(momentum.shape, jnp.float32)
-    block = pltpu.VMEM(momentum.shape, jnp.float32)
-    return pl.pallas_call(
-        state_kernel,
-        in_specs=[pl.BlockSpec(memory_space=pltpu.VMEM)] + [ANY] * 4,
-        out_shape=(
-            shape,
-            shape,
-            pltpu.VMEM(inner.shape, inner.dtype),
-            pltpu.VMEM((8, 128), jnp.float32),
-        ),
-        scratch_shapes=[block, block, block, pltpu.SemaphoreType.DMA((4,))],
-        compiler_params=pltpu.CompilerParams(vmem_limit_bytes=32 * MIB),
-        name="state",
-    )(total, *map(hbm, (delta, momentum, params, inner)))
+    copy.wait()
+
+
+def stage(total, inner):
+    return pl.pallas_call(
+        stage_kernel,
+        in_specs=[pl.BlockSpec(memory_space=pltpu.VMEM), ANY],
+        out_shape=(pltpu.VMEM(inner.shape, inner.dtype), pltpu.VMEM((8, 128), jnp.float32)),
+        scratch_shapes=[pltpu.SemaphoreType.DMA],
+        compiler_params=pltpu.CompilerParams(vmem_limit_bytes=32 * MIB),
+        name="stage",
+    )(total, hbm(inner))
 
 
 def merge_kernel(total_ref, grads_ref, inner_ref, global_ref, out_hbm, out_ref, sems):
     root_mean = jnp.sqrt(total_ref[:1, :1] / ENTRIES + 1e-6)
-    clip = jnp.minimum(1.0, 0.02 / root_mean)
+    share = 0.4 * jnp.minimum(1.0, 0.02 / root_mean)
     copies = []
     for c in range(REPLICAS):
         cols = pl.ds(c * 256, 256)
-        clipped = grads_ref[:, cols].astype(jnp.float32) * clip
-        master = inner_ref[:, cols].astype(jnp.float32)
-        stepped = master - 0.8 * (clipped + 0.2 * master)
-        mean = 0.5 * stepped + 0.5 * global_ref[c].astype(jnp.float32)
-        out_ref[:, cols] = mean.astype(jnp.bfloat16)
-        if c % 3 == 2:
-            cols = pl.ds((c - 2) * 256, 768)
-            copies.append(pltpu.make_async_copy(out_ref.at[:, cols], out_hbm.at[:, cols], sems.at[c // 3]))
+        kept = 0.42 * inner_ref[:, cols].astype(jnp.float32) - share * grads_ref[:, cols].astype(jnp.float32)
+        out_ref[:, cols] = (kept + 0.5 * global_ref[c].astype(jnp.float32)).astype(jnp.bfloat16)
+        if c % 2 == 1:
+            cols = pl.ds((c - 1) * 256, 512)
+            copies.append(pltpu.make_async_copy(out_ref.at[:, cols], out_hbm.at[:, cols], sems.at[c // 2]))
             copies[-1].start()
     for copy in copies:
         copy.wait()
@@ -260,7 +226,7 @@
         merge_kernel,
         out_specs=ANY,
         out_shape=jax.ShapeDtypeStruct(inner.shape, jnp.bfloat16),
-        scratch_shapes=[pltpu.VMEM(inner.shape, jnp.bfloat16), pltpu.SemaphoreType.DMA((4,))],
+        scratch_shapes=[pltpu.VMEM(inner.shape, jnp.bfloat16), pltpu.SemaphoreType.DMA((6,))],
         compiler_params=pltpu.CompilerParams(vmem_limit_bytes=32 * MIB),
         name="merge",
     )(total, grads, inner, global_parts)
@@ -268,17 +234,16 @@
 
 def per_device(gate_pre, up_pre, out_grad, inner_params, global_params, outer_momentum, pair_codes, code_scales):
     pseudo, order = unpack(pair_codes[0], code_scales[0].T)
-    grads, total, momentum, params = gradients(order, gate_pre.T, up_pre.T, out_grad, outer_momentum, global_params)
     parts = lax.all_to_all(pseudo.reshape((REPLICAS,) + pseudo.shape[2:]), REP, 0, 0, tiled=True)
+    grads, total, momentum, params = gradients(
+        order, gate_pre.T, up_pre.T, out_grad, outer_momentum, global_params
+    )
+    total = lax.psum(lax.psum(total, "core"), "zh")
+    global_bf, new_global, new_momentum, total = update(parts, momentum, params, total)
+    global_parts = lax.all_to_all(global_bf, REP, 0, 0, tiled=True)
+    inner, total = stage(total, inner_params[0])
     total = lax.psum(total, "y")
-    global_bf, delta, total = update(parts, momentum, params, total)
-    run_parts = lax.all_to_all(global_bf, "zl", 0, 0, tiled=True)
-    total = lax.psum(total, "core")
-    new_global, new_momentum, inner, total = state(delta, outer_momentum, global_params, total, inner_params[0])
-    run_parts, total = repeat(run_parts, total)
-    global_parts = lax.all_to_all(run_parts, "x", 0, 0, tiled=True)
-    total = lax.psum(total, "zh")
-    merged = merge(total, grads, inner, global_parts.reshape((REPLICAS,) + global_parts.shape[2:]))
+    merged = merge(total, grads, inner, global_parts)
     return (merged[None], new_global, new_momentum)
 
 

time: 72.5 us -> 71.5 us (0.986)
  blocking collectives: 35.8 us -> 41.6 us
  starting transfers between devices: 21.6 us -> 18.5 us
  Pallas kernels: 13 us -> 10.4 us
  waiting for transfers between devices: 1.07 us -> 0.01 us
    psum x1, blocking collectives: 14.2 us -> 17.6 us  [per_device(): total = lax.psum(total, 'y')]
    all_to_all x2 -> x1, starting transfers between devices: 8.49 us -> 5.37 us  [per_device(): global_parts = lax.all_to_all(global_bf, REP, 0, 0, tiled=True)]
    psum x2, blocking collectives: 21.6 us -> 24 us  [per_device(): total = lax.psum(lax.psum(total, 'core'), 'zh')]
    pallas_call x3 -> x2, Pallas kernels: 5.28 us -> 3.03 us  [the longest x1 1.75 us: update(): pl.pallas_call(update_kernel, out_specs=(ANY, ANY, ANY, vmem), out_shape=...]
    all_to_all x2 -> x1, waiting for transfers between devices: 1.07 us -> 0.01 us  [per_device(): global_parts = lax.all_to_all(global_bf, REP, 0, 0, tiled=True)]
  transfers between devices with their start and end apart: 3 -> 2, of which waited for: 1 -> 0; matrix products, arithmetic and copies ran while one was open for 0% -> 0% of each run, Pallas kernels for 8% -> 6%
where the time goes in v3:
time: 71.5 us; the launch traced here: 71.2 us
  blocking collectives  41.6 us (58%)
  starting transfers between devices  18.5 us (26%)
  Pallas kernels  10.4 us (15%)
    psum x2, blocking collectives, per_device(): total = lax.psum(lax.psum(total, 'core'), 'zh')  24 us
    psum x1, blocking collectives, per_device(): total = lax.psum(total, 'y')  17.6 us
    all_to_all x1, starting transfers between devices, per_device(): lax.all_to_all(pseudo.reshape((REPLICAS,) + pseudo.shape[2:]), REP, 0, 0,...  13.1 us
    all_to_all x1, starting transfers between devices, per_device(): global_parts = lax.all_to_all(global_bf, REP, 0, 0, tiled=True)  5.37 us
    pallas_call x1, Pallas kernels, gradients(): pl.pallas_call(gradients_kernel, in_specs=[pl.BlockSpec(memory_space=pltp...  3.1 us
    pallas_call x1, Pallas kernels, unpack(): pl.pallas_call(unpack_kernel, in_specs=[ANY, ANY], out_specs=(ANY, pl.Blo...  2.69 us
    pallas_call x1, Pallas kernels, update(): pl.pallas_call(update_kernel, out_specs=(ANY, ANY, ANY, vmem), out_shape=...  1.75 us
    pallas_call x1, Pallas kernels, merge(): pl.pallas_call(merge_kernel, out_specs=ANY, out_shape=jax.ShapeDtypeStruc...  1.61 us
  transfers between devices with their start and end apart: 2, of which 0 were waited for; matrix products, arithmetic and copies ran while one was open for 0% of the time, Pallas kernels for 6%

profile of v3, /device:TPU:2, one launch (start us, length us, event | category | flops | bytes accessed | tf_op | source)
XLA Modules:
  0.0 71.2 jit_solution(12154535946375739577)
XLA Ops:
  0.6 2.7 %unpack.1 = (bf16[4,3,192,256]{3,2,1,0:T(8,128)(2,1)}, f32[8,128]{1,0:T(8,128)S(1)}) custom-call(s32[192,1536]{1,0:T(8,128)} %bitcast.9, f32[24,192]{1,0:T(8,128)} %bitcast.15), custom_call_target="tpu_custom_call" | custom-call | tf_op jit(solution)/shard_map/unpack/pallas_call | solution.py:55
  3.3 13.1 %all-to-all-start = ((bf16[12,192,256]{2,1,0:T(8,128)(2,1)}), bf16[12,192,256]{2,1,0:T(8,128)(2,1)S(1)}, u32[]{:S(2)}, u32[]{:S(2)}) async-start(bf16[12,192,256]{2,1,0:T(8,128)(2,1)} %bitcast.11), calls=%async_computation | async-start | bytes 2359296 | tf_op jit(solution)/shard_map/all_to_all | solution.py:237
  16.4 3.1 %gradients.1 = (bf16[192,3072]{1,0:T(8,128)(2,1)S(1)}, f32[8,128]{1,0:T(8,128)S(1)}, f32[192,256]{1,0:T(8,128)S(1)}, f32[192,256]{1,0:T(8,128)S(1)}) custom-call(f32[8,128]{1,0:T(8,128)S(1)} %get-tuple-element.16.order_ref, bf16[192,512]{1,0:T(8,128)(2,1)} %bitcast.13, bf16[192,512]{1,0:T(8,128)(2,1)} %bitcast.14, bf16[512,3072]{1,0:T(8,128)(2,1)} %out_grad_hbm.1, ...), custom_call_target="tpu_custom_call" | custom-call | flops 603979776 | bytes 6000000 | tf_op jit(solution)/shard_map/gradients/pallas_call | solution.py:118
  19.6 2.5 %psum.21 = f32[8,128]{1,0:T(8,128)S(1)} all-reduce(f32[8,128]{1,0:T(8,128)S(1)} %get-tuple-element.17), channel_id=1, replica_groups=mesh['x'=4,'zl'=3,'zh'=4,'y'=8,'core'=2] {'core'}, use_global_device_ids=true, to_apply=%region_0.0 | all-reduce | flops 1024 | bytes 8192 | tf_op jit(solution)/shard_map/psum | solution.py:241
  22.0 21.5 %psum.22.total_ref = f32[8,128]{1,0:T(8,128)S(1)} all-reduce(f32[8,128]{1,0:T(8,128)S(1)} %psum.21), channel_id=1, replica_groups=mesh['x'=4,'zl'=3,'zh'=4,'y'=8,'core'=2] {'zh'}, use_global_device_ids=true, to_apply=%region_1.0 | all-reduce | flops 1024 | bytes 8192 | tf_op jit(solution)/shard_map/psum | solution.py:241
  43.5 0.0 all-to-all-done.parts_ref
  43.5 1.8 %update.1 = (bf16[12,192,256]{2,1,0:T(8,128)(2,1)}, f32[192,256]{1,0:T(8,128)}, f32[192,256]{1,0:T(8,128)}, f32[8,128]{1,0:T(8,128)S(1)}) custom-call(bf16[12,192,256]{2,1,0:T(8,128)(2,1)S(1)} %all-to-all-done.parts_ref, f32[8,128]{1,0:T(8,128)S(1)} %psum.22.total_ref, f32[192,256]{1,0:T(8,128)S(1)} %get-tuple-element.18.momentum_ref, ...), custom_call_target="tpu_custom_call" | custom-call | tf_op jit(solution)/shard_map/update/pallas_call | solution.py:173
  45.3 5.4 %all-to-all-start.1 = ((bf16[12,192,256]{2,1,0:T(8,128)(2,1)}), bf16[12,192,256]{2,1,0:T(8,128)(2,1)S(1)}, u32[]{:S(2)}, u32[]{:S(2)}) async-start(bf16[12,192,256]{2,1,0:T(8,128)(2,1)} %get-tuple-element.24), calls=%async_computation.1 | async-start | bytes 2359296 | tf_op jit(solution)/shard_map/all_to_all | solution.py:243
  50.7 1.3 %stage.1 = (bf16[192,3072]{1,0:T(8,128)(2,1)S(1)}, f32[8,128]{1,0:T(8,128)S(1)}) custom-call(f32[8,128]{1,0:T(8,128)S(1)} %get-tuple-element.20.total_ref, bf16[192,3072]{1,0:T(8,128)(2,1)} %bitcast.10), custom_call_target="tpu_custom_call" | custom-call | tf_op jit(solution)/shard_map/stage/pallas_call | solution.py:198
  51.9 17.6 %psum.23.total_ref = f32[8,128]{1,0:T(8,128)S(1)} all-reduce(f32[8,128]{1,0:T(8,128)S(1)} %get-tuple-element.21), channel_id=1, replica_groups=mesh['x'=4,'zl'=3,'zh'=4,'y'=8,'core'=2] {'y'}, use_global_device_ids=true, to_apply=%region_2.0 | all-reduce | flops 1024 | bytes 8192 | tf_op jit(solution)/shard_map/psum | solution.py:245
  69.6 0.0 all-to-all-done.1.global_ref
  69.6 1.6 %merge.1 = bf16[192,3072]{1,0:T(8,128)(2,1)} custom-call(f32[8,128]{1,0:T(8,128)S(1)} %psum.23.total_ref, bf16[192,3072]{1,0:T(8,128)(2,1)S(1)} %get-tuple-element.22.grads_ref, bf16[192,3072]{1,0:T(8,128)(2,1)S(1)} %get-tuple-element.23.inner_ref, bf16[12,192,256]{2,1,0:T(8,128)(2,1)S(1)} %all-to-all-done.1.global_ref), custom_call_target="tpu_custom_call" | custom-call | tf_op jit(solution)/shard_map/merge/pallas_call | solution.py:225
Async XLA Ops:
  3.3 40.2 %all-to-all-start = ((bf16[12,192,256]{2,1,0:T(8,128)(2,1)}), bf16[12,192,256]{2,1,0:T(8,128)(2,1)S(1)}, u32[]{:S(2)}, u32[]{:S(2)}) async-start(bf16[12,192,256]{2,1,0:T(8,128)(2,1)} %bitcast.11), calls=%async_computation | async-start | bytes 2359296 | tf_op jit(solution)/shard_map/all_to_all | solution.py:237
  45.3 24.3 %all-to-all-start.1 = ((bf16[12,192,256]{2,1,0:T(8,128)(2,1)}), bf16[12,192,256]{2,1,0:T(8,128)(2,1)S(1)}, u32[]{:S(2)}, u32[]{:S(2)}) async-start(bf16[12,192,256]{2,1,0:T(8,128)(2,1)} %get-tuple-element.24), calls=%async_computation.1 | async-start | bytes 2359296 | tf_op jit(solution)/shard_map/all_to_all | solution.py:243

commit v4 on v3

--- a/solution.py
+++ b/solution.py
@@ -1,3 +1,5 @@
+import functools
+
 import jax
 import jax.numpy as jnp
 from jax import lax
@@ -17,7 +19,7 @@
     return pltpu.with_memory_space_constraint(x, pltpu.HBM)
 
 
-def unpack_kernel(words_hbm, scales_hbm, out_hbm, order_ref, words_ref, scales_ref, out_ref, sems):
+def unpack_kernel(words_hbm, scales_hbm, after_ref, out_hbm, order_ref, words_ref, scales_ref, out_ref, sems):
     steps, per_step, rows, _ = out_ref.shape
     span = per_step * 128
     copies_in = [pltpu.make_async_copy(scales_hbm, scales_ref, sems.at[0])]
@@ -49,12 +51,12 @@
         copy.wait()
 
 
-def unpack(words, scales_t):
+def unpack(words, scales_t, after):
     rows, width = words.shape
     shape = (4, REPLICAS // 4, rows, 256)
     return pl.pallas_call(
         unpack_kernel,
-        in_specs=[ANY, ANY],
+        in_specs=[ANY, ANY, pl.BlockSpec(memory_space=pltpu.VMEM)],
         out_specs=(ANY, pl.BlockSpec(memory_space=pltpu.VMEM)),
         out_shape=(
             pltpu.HBM(shape, jnp.bfloat16),
@@ -68,10 +70,10 @@
         ],
         compiler_params=pltpu.CompilerParams(vmem_limit_bytes=32 * MIB),
         name="unpack",
-    )(hbm(words), hbm(scales_t))
-
-
-def gradients_kernel(
+    )(hbm(words), hbm(scales_t), after)
+
+
+def gradients_body(
     order_ref, gate_hbm, up_hbm, out_grad_hbm, momentum_hbm, params_hbm,
     grads_ref, total_ref, momentum_ref, params_ref,
     gate_ref, up_ref, out_grad_ref, sems,
@@ -112,12 +114,22 @@
         copy.wait()
 
 
-def gradients(order, gate_t, up_t, out_grad, momentum, params):
+def gradients_kernel(core, order_ref, *refs):
+    if core == 1:
+        refs = refs[4:]
+
+    @pl.when(lax.axis_index("core") == core)
+    def _():
+        gradients_body(order_ref, *refs)
+
+
+def gradients(core, order, earlier, gate_t, up_t, out_grad, momentum, params):
     rows, tokens = gate_t.shape
     width = out_grad.shape[1]
     return pl.pallas_call(
-        gradients_kernel,
-        in_specs=[pl.BlockSpec(memory_space=pltpu.VMEM)] + [ANY] * 5,
+        functools.partial(gradients_kernel, core),
+        in_specs=[pl.BlockSpec(memory_space=pltpu.VMEM)] * (1 + len(earlier)) + [ANY] * 5,
+        input_output_aliases={1 + i: i for i in range(len(earlier))},
         out_shape=(
             pltpu.VMEM((rows, width), jnp.bfloat16),
             pltpu.VMEM((8, 128), jnp.float32),
@@ -135,7 +147,7 @@
             flops=2 * rows * width * tokens, bytes_accessed=6_000_000, transcendentals=rows * tokens
         ),
         name="gradients",
-    )(order, *map(hbm, (gate_t, up_t, out_grad, momentum, params)))
+    )(order, *earlier, *map(hbm, (gate_t, up_t, out_grad, momentum, params)))
 
 
 def update_kernel(parts_ref, total_ref, momentum_ref, params_ref,
@@ -232,17 +244,31 @@
     )(total, grads, inner, global_parts)
 
 
+def run_sum(total):
+    zh, y = lax.axis_size("zh"), lax.axis_size("y")
+    groups = [[2 * (i * y + j) + 1 for i in range(zh)] for j in range(y)]
+    groups += [[2 * (i * y + j + k) for k in range(zh)] for i in range(zh) for j in range(0, y, zh)]
+    total = lax.psum(total, FSDP, axis_index_groups=groups)
+    return jnp.where(lax.axis_index("core") == 1, total, 0.0)
+
+
+def crossed_sum(total, axis):
+    n = lax.axis_size(axis)
+    groups = [[2 * i + (i + p) % 2 for i in range(n)] for p in range(2)]
+    return lax.psum(total, (axis, "core"), axis_index_groups=groups)
+
+
 def per_device(gate_pre, up_pre, out_grad, inner_params, global_params, outer_momentum, pair_codes, code_scales):
-    pseudo, order = unpack(pair_codes[0], code_scales[0].T)
+    operands = (gate_pre.T, up_pre.T, out_grad, outer_momentum, global_params)
+    early = gradients(0, jnp.zeros((8, 128), jnp.float32), (), *operands)
+    pseudo, order = unpack(pair_codes[0], code_scales[0].T, early[1])
     parts = lax.all_to_all(pseudo.reshape((REPLICAS,) + pseudo.shape[2:]), REP, 0, 0, tiled=True)
-    grads, total, momentum, params = gradients(
-        order, gate_pre.T, up_pre.T, out_grad, outer_momentum, global_params
-    )
-    total = lax.psum(lax.psum(total, "core"), "zh")
+    grads, total, momentum, params = gradients(1, order, early, *operands)
+    total = run_sum(lax.psum(total, "core"))
     global_bf, new_global, new_momentum, total = update(parts, momentum, params, total)
     global_parts = lax.all_to_all(global_bf, REP, 0, 0, tiled=True)
     inner, total = stage(total, inner_params[0])
-    total = lax.psum(total, "y")
+    total = crossed_sum(lax.psum(total, "core"), "y")
     merged = merge(total, grads, inner, global_parts)
     return (merged[None], new_global, new_momentum)
 

time: 71.5 us -> 66.7 us (0.933)
  the two profiles are of different devices: /device:TPU:2 before, /device:TPU:1 now
where the time goes in v4:
time: 66.7 us; the launch traced here: 66.4 us
  blocking collectives  42.8 us (64%)
  starting transfers between devices  12.3 us (18%)
  Pallas kernels  10.5 us (16%)
  between operations  0.7 us (1%)
    psum x1, blocking collectives, run_sum(): total = lax.psum(total, FSDP, axis_index_groups=groups)  16.5 us
    psum x1, blocking collectives, crossed_sum(): return lax.psum(total, (axis, 'core'), axis_index_groups=groups)  15.9 us
    all_to_all x1, starting transfers between devices, per_device(): lax.all_to_all(pseudo.reshape((REPLICAS,) + pseudo.shape[2:]), REP, 0, 0,...  8.51 us
    psum x1, blocking collectives, per_device(): total = run_sum(lax.psum(total, 'core'))  7.86 us
    all_to_all x1, starting transfers between devices, per_device(): global_parts = lax.all_to_all(global_bf, REP, 0, 0, tiled=True)  3.8 us
    pallas_call x2, Pallas kernels, gradients(): pl.pallas_call(functools.partial(gradients_kernel, core), in_specs=[pl.Bl...  3.22 us
    pallas_call x1, Pallas kernels, unpack(): pl.pallas_call(unpack_kernel, in_specs=[ANY, ANY, pl.BlockSpec(memory_spa...  2.69 us
    psum x1, blocking collectives, per_device(): total = crossed_sum(lax.psum(total, 'core'), 'y')  2.49 us
  transfers between devices with their start and end apart: 2, of which 0 were waited for; matrix products, arithmetic and copies ran while one was open for 0% of the time, Pallas kernels for 7%

profile of v4, /device:TPU:1, one launch (start us, length us, event | category | flops | bytes accessed | tf_op | source)
XLA Modules:
  0.0 66.4 jit_solution(2936495110113744605)
XLA Ops:
  0.6 0.1 gradients.2
  0.8 2.7 %unpack.1 = (bf16[4,3,192,256]{3,2,1,0:T(8,128)(2,1)}, f32[8,128]{1,0:T(8,128)S(1)}) custom-call(s32[192,1536]{1,0:T(8,128)} %bitcast.9, f32[24,192]{1,0:T(8,128)} %bitcast.17, f32[8,128]{1,0:T(8,128)S(1)} %get-tuple-element.19.after_ref.refs_1_), custom_call_target="tpu_custom_call" | custom-call | tf_op jit(solution)/shard_map/unpack/pallas_call | solution.py:57
  3.5 8.5 %all-to-all-start = ((bf16[12,192,256]{2,1,0:T(8,128)(2,1)}), bf16[12,192,256]{2,1,0:T(8,128)(2,1)S(1)}, u32[]{:S(2)}, u32[]{:S(2)}) async-start(bf16[12,192,256]{2,1,0:T(8,128)(2,1)} %bitcast.11), calls=%async_computation | async-start | bytes 2359296 | tf_op jit(solution)/shard_map/all_to_all | solution.py:265
  12.0 3.1 %gradients.3 = (bf16[192,3072]{1,0:T(8,128)(2,1)S(1)}, f32[8,128]{1,0:T(8,128)S(1)}, f32[192,256]{1,0:T(8,128)S(1)}, f32[192,256]{1,0:T(8,128)S(1)}) custom-call(f32[8,128]{1,0:T(8,128)S(1)} %get-tuple-element.21.order_ref, bf16[192,3072]{1,0:T(8,128)(2,1)S(1)} %get-tuple-element.22.refs_0_, ...), custom_call_target="tpu_custom_call", output_to_operand_aliasing={{0}: (1, {}), {1}: (2, {}), {2}: (3, {}), {3}: (4, {})} | custom-call | flops 603979776 | bytes 6000000 | tf_op jit(solution)/shard_map/gradients/pallas_call | solution.py:129
  15.1 7.9 %psum.28 = f32[8,128]{1,0:T(8,128)S(1)} all-reduce(f32[8,128]{1,0:T(8,128)S(1)} %get-tuple-element.25), channel_id=1, replica_groups=mesh['x'=4,'zl'=3,'zh'=4,'y'=8,'core'=2] {'core'}, use_global_device_ids=true, to_apply=%region_0.0 | all-reduce | flops 1024 | bytes 8192 | tf_op jit(solution)/shard_map/psum | solution.py:267
  23.0 16.5 %psum.29 = f32[8,128]{1,0:T(8,128)S(1)} all-reduce(f32[8,128]{1,0:T(8,128)S(1)} %psum.28), channel_id=1, replica_groups={{1,17,33,49},{3,19,35,51},{5,21,37,53},{7,23,39,55},{9,25,41,57},{11,27..., use_global_device_ids=true, to_apply=%region_1.0 | all-reduce | flops 1024 | bytes 8192 | tf_op jit(solution)/shard_map/psum | solution.py:251
  39.5 0.0 all-to-all-done.parts_ref
  39.5 1.7 %update.1 = (bf16[12,192,256]{2,1,0:T(8,128)(2,1)}, f32[192,256]{1,0:T(8,128)}, f32[192,256]{1,0:T(8,128)}, f32[8,128]{1,0:T(8,128)S(1)}) custom-call(bf16[12,192,256]{2,1,0:T(8,128)(2,1)S(1)} %all-to-all-done.parts_ref, f32[8,128]{1,0:T(8,128)S(1)} %broadcast_select_fusion.total_ref, f32[192,256]{1,0:T(8,128)S(1)} %get-tuple-element.26.momentum_ref, ...), custom_call_target="tpu_custom_call" | custom-call | tf_op jit(solution)/shard_map/update/pallas_call | solution.py:185
  41.2 3.8 %all-to-all-start.1 = ((bf16[12,192,256]{2,1,0:T(8,128)(2,1)}), bf16[12,192,256]{2,1,0:T(8,128)(2,1)S(1)}, u32[]{:S(2)}, u32[]{:S(2)}) async-start(bf16[12,192,256]{2,1,0:T(8,128)(2,1)} %get-tuple-element.32), calls=%async_computation.1 | async-start | bytes 2359296 | tf_op jit(solution)/shard_map/all_to_all | solution.py:269
  45.0 1.3 %stage.1 = (bf16[192,3072]{1,0:T(8,128)(2,1)S(1)}, f32[8,128]{1,0:T(8,128)S(1)}) custom-call(f32[8,128]{1,0:T(8,128)S(1)} %get-tuple-element.28.total_ref, bf16[192,3072]{1,0:T(8,128)(2,1)} %bitcast.10), custom_call_target="tpu_custom_call" | custom-call | tf_op jit(solution)/shard_map/stage/pallas_call | solution.py:210
  46.3 2.5 %psum.30 = f32[8,128]{1,0:T(8,128)S(1)} all-reduce(f32[8,128]{1,0:T(8,128)S(1)} %get-tuple-element.29), channel_id=1, replica_groups=mesh['x'=4,'zl'=3,'zh'=4,'y'=8,'core'=2] {'core'}, use_global_device_ids=true, to_apply=%region_2.3 | all-reduce | flops 1024 | bytes 8192 | tf_op jit(solution)/shard_map/psum | solution.py:271
  48.8 15.9 %psum.31.total_ref = f32[8,128]{1,0:T(8,128)S(1)} all-reduce(f32[8,128]{1,0:T(8,128)S(1)} %psum.30), channel_id=1, replica_groups={{0,3,4,7,8,11,12,15},{1,2,5,6,9,10,13,14},{16,19,20,23,24,27,28,31},{17..., use_global_device_ids=true, to_apply=%region_3.4 | all-reduce | flops 1024 | bytes 8192 | tf_op jit(solution)/shard_map/psum | solution.py:258
  64.8 0.0 all-to-all-done.1.global_ref
  64.8 1.6 %merge.1 = bf16[192,3072]{1,0:T(8,128)(2,1)} custom-call(f32[8,128]{1,0:T(8,128)S(1)} %psum.31.total_ref, bf16[192,3072]{1,0:T(8,128)(2,1)S(1)} %get-tuple-element.30.grads_ref, bf16[192,3072]{1,0:T(8,128)(2,1)S(1)} %get-tuple-element.31.inner_ref, bf16[12,192,256]{2,1,0:T(8,128)(2,1)S(1)} %all-to-all-done.1.global_ref), custom_call_target="tpu_custom_call" | custom-call | tf_op jit(solution)/shard_map/merge/pallas_call | solution.py:237
  (2 shorter events, 0.0 us)
Async XLA Ops:
  3.5 36.0 %all-to-all-start = ((bf16[12,192,256]{2,1,0:T(8,128)(2,1)}), bf16[12,192,256]{2,1,0:T(8,128)(2,1)S(1)}, u32[]{:S(2)}, u32[]{:S(2)}) async-start(bf16[12,192,256]{2,1,0:T(8,128)(2,1)} %bitcast.11), calls=%async_computation | async-start | bytes 2359296 | tf_op jit(solution)/shard_map/all_to_all | solution.py:265
  41.2 23.5 %all-to-all-start.1 = ((bf16[12,192,256]{2,1,0:T(8,128)(2,1)}), bf16[12,192,256]{2,1,0:T(8,128)(2,1)S(1)}, u32[]{:S(2)}, u32[]{:S(2)}) async-start(bf16[12,192,256]{2,1,0:T(8,128)(2,1)} %get-tuple-element.32), calls=%async_computation.1 | async-start | bytes 2359296 | tf_op jit(solution)/shard_map/all_to_all | solution.py:269

commit v5 on v4

--- a/solution.py
+++ b/solution.py
@@ -248,14 +248,7 @@
     zh, y = lax.axis_size("zh"), lax.axis_size("y")
     groups = [[2 * (i * y + j) + 1 for i in range(zh)] for j in range(y)]
     groups += [[2 * (i * y + j + k) for k in range(zh)] for i in range(zh) for j in range(0, y, zh)]
-    total = lax.psum(total, FSDP, axis_index_groups=groups)
-    return jnp.where(lax.axis_index("core") == 1, total, 0.0)
-
-
-def crossed_sum(total, axis):
-    n = lax.axis_size(axis)
-    groups = [[2 * i + (i + p) % 2 for i in range(n)] for p in range(2)]
-    return lax.psum(total, (axis, "core"), axis_index_groups=groups)
+    return lax.psum(total, FSDP, axis_index_groups=groups)
 
 
 def per_device(gate_pre, up_pre, out_grad, inner_params, global_params, outer_momentum, pair_codes, code_scales):
@@ -268,7 +261,8 @@
     global_bf, new_global, new_momentum, total = update(parts, momentum, params, total)
     global_parts = lax.all_to_all(global_bf, REP, 0, 0, tiled=True)
     inner, total = stage(total, inner_params[0])
-    total = crossed_sum(lax.psum(total, "core"), "y")
+    total = jnp.where(lax.axis_index("core") == 1, lax.psum(total, "y"), 0.0)
+    total = lax.psum(total, "core")
     merged = merge(total, grads, inner, global_parts)
     return (merged[None], new_global, new_momentum)
 

time: 66.7 us -> 66.2 us (level); the launches traced: 66.4 us -> 65.2 us
  blocking collectives: 42.8 us -> 41.6 us
    psum x3, blocking collectives: 34.9 us -> 33.8 us  [the longest x1 16.5 us: run_sum(): return lax.psum(total, FSDP, axis_index_groups=groups)]
where the time goes in v5:
time: 66.2 us; the launch traced here: 65.2 us
  blocking collectives  41.6 us (63%)
  starting transfers between devices  12.3 us (19%)
  Pallas kernels  10.5 us (16%)
  between operations  0.7 us (1%)
    psum x1, blocking collectives, run_sum(): return lax.psum(total, FSDP, axis_index_groups=groups)  16.5 us
    psum x1, blocking collectives, per_device(): total = jnp.where(lax.axis_index('core') == 1, lax.psum(total, 'y'), 0.0)  14.8 us
    all_to_all x1, starting transfers between devices, per_device(): lax.all_to_all(pseudo.reshape((REPLICAS,) + pseudo.shape[2:]), REP, 0, 0,...  8.51 us
    psum x1, blocking collectives, per_device(): total = run_sum(lax.psum(total, 'core'))  7.86 us
    all_to_all x1, starting transfers between devices, per_device(): global_parts = lax.all_to_all(global_bf, REP, 0, 0, tiled=True)  3.8 us
    pallas_call x2, Pallas kernels, gradients(): pl.pallas_call(functools.partial(gradients_kernel, core), in_specs=[pl.Bl...  3.22 us
    pallas_call x1, Pallas kernels, unpack(): pl.pallas_call(unpack_kernel, in_specs=[ANY, ANY, pl.BlockSpec(memory_spa...  2.69 us
    psum x1, blocking collectives, per_device(): total = lax.psum(total, 'core')  2.49 us
  transfers between devices with their start and end apart: 2, of which 0 were waited for; matrix products, arithmetic and copies ran while one was open for 0% of the time, Pallas kernels for 7%

profile of v5, /device:TPU:1, one launch (start us, length us, event | category | flops | bytes accessed | tf_op | source)
XLA Modules:
  0.0 65.2 jit_solution(563711007565598603)
XLA Ops:
  0.6 0.1 gradients.2
  0.8 2.7 %unpack.1 = (bf16[4,3,192,256]{3,2,1,0:T(8,128)(2,1)}, f32[8,128]{1,0:T(8,128)S(1)}) custom-call(s32[192,1536]{1,0:T(8,128)} %bitcast.9, f32[24,192]{1,0:T(8,128)} %bitcast.17, f32[8,128]{1,0:T(8,128)S(1)} %get-tuple-element.19.after_ref.refs_1_), custom_call_target="tpu_custom_call" | custom-call | tf_op jit(solution)/shard_map/unpack/pallas_call | solution.py:57
  3.5 8.5 %all-to-all-start = ((bf16[12,192,256]{2,1,0:T(8,128)(2,1)}), bf16[12,192,256]{2,1,0:T(8,128)(2,1)S(1)}, u32[]{:S(2)}, u32[]{:S(2)}) async-start(bf16[12,192,256]{2,1,0:T(8,128)(2,1)} %bitcast.11), calls=%async_computation | async-start | bytes 2359296 | tf_op jit(solution)/shard_map/all_to_all | solution.py:258
  12.0 3.1 %gradients.3 = (bf16[192,3072]{1,0:T(8,128)(2,1)S(1)}, f32[8,128]{1,0:T(8,128)S(1)}, f32[192,256]{1,0:T(8,128)S(1)}, f32[192,256]{1,0:T(8,128)S(1)}) custom-call(f32[8,128]{1,0:T(8,128)S(1)} %get-tuple-element.21.order_ref, bf16[192,3072]{1,0:T(8,128)(2,1)S(1)} %get-tuple-element.22.refs_0_, ...), custom_call_target="tpu_custom_call", output_to_operand_aliasing={{0}: (1, {}), {1}: (2, {}), {2}: (3, {}), {3}: (4, {})} | custom-call | flops 603979776 | bytes 6000000 | tf_op jit(solution)/shard_map/gradients/pallas_call | solution.py:129
  15.1 7.9 %psum.28 = f32[8,128]{1,0:T(8,128)S(1)} all-reduce(f32[8,128]{1,0:T(8,128)S(1)} %get-tuple-element.25), channel_id=1, replica_groups=mesh['x'=4,'zl'=3,'zh'=4,'y'=8,'core'=2] {'core'}, use_global_device_ids=true, to_apply=%region_0.0 | all-reduce | flops 1024 | bytes 8192 | tf_op jit(solution)/shard_map/psum | solution.py:260
  23.0 16.5 %psum.29.total_ref = f32[8,128]{1,0:T(8,128)S(1)} all-reduce(f32[8,128]{1,0:T(8,128)S(1)} %psum.28), channel_id=1, replica_groups={{1,17,33,49},{3,19,35,51},{5,21,37,53},{7,23,39,55},{9,25,41,57},{11,27..., use_global_device_ids=true, to_apply=%region_1.0 | all-reduce | flops 1024 | bytes 8192 | tf_op jit(solution)/shard_map/psum | solution.py:251
  39.5 0.0 all-to-all-done.parts_ref
  39.5 1.7 %update.1 = (bf16[12,192,256]{2,1,0:T(8,128)(2,1)}, f32[192,256]{1,0:T(8,128)}, f32[192,256]{1,0:T(8,128)}, f32[8,128]{1,0:T(8,128)S(1)}) custom-call(bf16[12,192,256]{2,1,0:T(8,128)(2,1)S(1)} %all-to-all-done.parts_ref, f32[8,128]{1,0:T(8,128)S(1)} %psum.29.total_ref, f32[192,256]{1,0:T(8,128)S(1)} %get-tuple-element.26.momentum_ref, ...), custom_call_target="tpu_custom_call" | custom-call | tf_op jit(solution)/shard_map/update/pallas_call | solution.py:185
  41.2 3.8 %all-to-all-start.1 = ((bf16[12,192,256]{2,1,0:T(8,128)(2,1)}), bf16[12,192,256]{2,1,0:T(8,128)(2,1)S(1)}, u32[]{:S(2)}, u32[]{:S(2)}) async-start(bf16[12,192,256]{2,1,0:T(8,128)(2,1)} %get-tuple-element.32), calls=%async_computation.1 | async-start | bytes 2359296 | tf_op jit(solution)/shard_map/all_to_all | solution.py:262
  45.0 1.3 %stage.1 = (bf16[192,3072]{1,0:T(8,128)(2,1)S(1)}, f32[8,128]{1,0:T(8,128)S(1)}) custom-call(f32[8,128]{1,0:T(8,128)S(1)} %get-tuple-element.28.total_ref, bf16[192,3072]{1,0:T(8,128)(2,1)} %bitcast.10), custom_call_target="tpu_custom_call" | custom-call | tf_op jit(solution)/shard_map/stage/pallas_call | solution.py:210
  46.3 14.8 %psum.30 = f32[8,128]{1,0:T(8,128)S(1)} all-reduce(f32[8,128]{1,0:T(8,128)S(1)} %get-tuple-element.29), channel_id=1, replica_groups=mesh['x'=4,'zl'=3,'zh'=4,'y'=8,'core'=2] {'y'}, use_global_device_ids=true, to_apply=%region_2.0 | all-reduce | flops 1024 | bytes 8192 | tf_op jit(solution)/shard_map/psum | solution.py:264
  61.1 2.5 %psum.31.total_ref = f32[8,128]{1,0:T(8,128)S(1)} all-reduce(f32[8,128]{1,0:T(8,128)S(1)} %broadcast_select_fusion), channel_id=1, replica_groups=mesh['x'=4,'zl'=3,'zh'=4,'y'=8,'core'=2] {'core'}, use_global_device_ids=true, to_apply=%region_3.4 | all-reduce | flops 1024 | bytes 8192 | tf_op jit(solution)/shard_map/psum | solution.py:265
  63.6 0.0 all-to-all-done.1.global_ref
  63.6 1.6 %merge.1 = bf16[192,3072]{1,0:T(8,128)(2,1)} custom-call(f32[8,128]{1,0:T(8,128)S(1)} %psum.31.total_ref, bf16[192,3072]{1,0:T(8,128)(2,1)S(1)} %get-tuple-element.30.grads_ref, bf16[192,3072]{1,0:T(8,128)(2,1)S(1)} %get-tuple-element.31.inner_ref, bf16[12,192,256]{2,1,0:T(8,128)(2,1)S(1)} %all-to-all-done.1.global_ref), custom_call_target="tpu_custom_call" | custom-call | tf_op jit(solution)/shard_map/merge/pallas_call | solution.py:237
  (2 shorter events, 0.0 us)
Async XLA Ops:
  3.5 36.0 %all-to-all-start = ((bf16[12,192,256]{2,1,0:T(8,128)(2,1)}), bf16[12,192,256]{2,1,0:T(8,128)(2,1)S(1)}, u32[]{:S(2)}, u32[]{:S(2)}) async-start(bf16[12,192,256]{2,1,0:T(8,128)(2,1)} %bitcast.11), calls=%async_computation | async-start | bytes 2359296 | tf_op jit(solution)/shard_map/all_to_all | solution.py:258
  41.2 22.4 %all-to-all-start.1 = ((bf16[12,192,256]{2,1,0:T(8,128)(2,1)}), bf16[12,192,256]{2,1,0:T(8,128)(2,1)S(1)}, u32[]{:S(2)}, u32[]{:S(2)}) async-start(bf16[12,192,256]{2,1,0:T(8,128)(2,1)} %get-tuple-element.32), calls=%async_computation.1 | async-start | bytes 2359296 | tf_op jit(solution)/shard_map/all_to_all | solution.py:262

commit v6 on v5

--- a/solution.py
+++ b/solution.py
@@ -155,21 +155,29 @@
     row = lax.broadcasted_iota(jnp.int32, (256, 256), 0)
     col = lax.broadcasted_iota(jnp.int32, (256, 256), 1)
     weave = ((row & 127) * 2 + (row >> 7) == col).astype(jnp.bfloat16)
-    delta = jnp.zeros(momentum_ref.shape, jnp.float32)
-    for c in range(REPLICAS):
-        delta += jnp.dot(parts_ref[c], weave, preferred_element_type=jnp.float32)
-    delta = delta * (1.0 / REPLICAS)
-    momentum = 0.9 * momentum_ref[...] + delta
-    new_global = params_ref[...] - 0.7 * (delta + 0.9 * momentum)
-    bf_ref[...] = new_global.astype(jnp.bfloat16)
-    copies = [pltpu.make_async_copy(bf_ref, bf_hbm.at[c], sems.at[c]) for c in range(REPLICAS)]
-    for copy in copies:
-        copy.start()
-    momentum_out_ref[...] = momentum
-    global_ref[...] = new_global
+    half = bf_ref.shape[0] // 2
+    copies = []
+    for h in range(2):
+        rows = pl.ds(h * half, half)
+        delta = jnp.zeros((half, momentum_ref.shape[1]), jnp.float32)
+        for c in range(REPLICAS):
+            delta += jnp.dot(parts_ref[c, rows, :], weave, preferred_element_type=jnp.float32)
+        delta = delta * (1.0 / REPLICAS)
+        momentum = 0.9 * momentum_ref[rows, :] + delta
+        new_global = params_ref[rows, :] - 0.7 * (delta + 0.9 * momentum)
+        bf_ref[rows, :] = new_global.astype(jnp.bfloat16)
+        sent = [
+            pltpu.make_async_copy(bf_ref.at[rows, :], bf_hbm.at[c, rows, :], sems.at[h * REPLICAS + c])
+            for c in range(REPLICAS)
+        ]
+        for copy in sent:
+            copy.start()
+        copies += sent
+        momentum_out_ref[rows, :] = momentum
+        global_ref[rows, :] = new_global
     outs = [
-        pltpu.make_async_copy(momentum_out_ref, momentum_hbm, sems.at[REPLICAS]),
-        pltpu.make_async_copy(global_ref, global_hbm, sems.at[REPLICAS + 1]),
+        pltpu.make_async_copy(momentum_out_ref, momentum_hbm, sems.at[2 * REPLICAS]),
+        pltpu.make_async_copy(global_ref, global_hbm, sems.at[2 * REPLICAS + 1]),
     ]
     for copy in outs:
         copy.start()
@@ -192,7 +200,7 @@
             pltpu.VMEM((rows, width), jnp.float32),
             pltpu.VMEM((rows, width), jnp.float32),
             pltpu.VMEM((rows, width), jnp.bfloat16),
-            pltpu.SemaphoreType.DMA((REPLICAS + 2,)),
+            pltpu.SemaphoreType.DMA((2 * REPLICAS + 2,)),
         ],
         compiler_params=pltpu.CompilerParams(vmem_limit_bytes=32 * MIB),
         name="update",

time: 66.2 us -> 66.5 us (level)
  no operation moved by 1% of the time
where the time goes in v6:
time: 66.5 us; the launch traced here: 65.5 us
  blocking collectives  41.6 us (63%)
  starting transfers between devices  12.3 us (18%)
  Pallas kernels  10.8 us (16%)
  between operations  0.7 us (1%)
    psum x1, blocking collectives, run_sum(): return lax.psum(total, FSDP, axis_index_groups=groups)  16.5 us
    psum x1, blocking collectives, per_device(): total = jnp.where(lax.axis_index('core') == 1, lax.psum(total, 'y'), 0.0)  14.8 us
    all_to_all x1, starting transfers between devices, per_device(): lax.all_to_all(pseudo.reshape((REPLICAS,) + pseudo.shape[2:]), REP, 0, 0,...  8.51 us
    psum x1, blocking collectives, per_device(): total = run_sum(lax.psum(total, 'core'))  7.86 us
    all_to_all x1, starting transfers between devices, per_device(): global_parts = lax.all_to_all(global_bf, REP, 0, 0, tiled=True)  3.8 us
    pallas_call x2, Pallas kernels, gradients(): pl.pallas_call(functools.partial(gradients_kernel, core), in_specs=[pl.Bl...  3.22 us
    pallas_call x1, Pallas kernels, unpack(): pl.pallas_call(unpack_kernel, in_specs=[ANY, ANY, pl.BlockSpec(memory_spa...  2.69 us
    psum x1, blocking collectives, per_device(): total = lax.psum(total, 'core')  2.49 us
  transfers between devices with their start and end apart: 2, of which 0 were waited for; matrix products, arithmetic and copies ran while one was open for 0% of the time, Pallas kernels for 7%

profile of v6, /device:TPU:1, one launch (start us, length us, event | category | flops | bytes accessed | tf_op | source)
XLA Modules:
  0.0 65.5 jit_solution(18287889011404725910)
XLA Ops:
  0.6 0.1 gradients.2
  0.8 2.7 %unpack.1 = (bf16[4,3,192,256]{3,2,1,0:T(8,128)(2,1)}, f32[8,128]{1,0:T(8,128)S(1)}) custom-call(s32[192,1536]{1,0:T(8,128)} %bitcast.9, f32[24,192]{1,0:T(8,128)} %bitcast.17, f32[8,128]{1,0:T(8,128)S(1)} %get-tuple-element.19.after_ref.refs_1_), custom_call_target="tpu_custom_call" | custom-call | tf_op jit(solution)/shard_map/unpack/pallas_call | solution.py:57
  3.5 8.5 %all-to-all-start = ((bf16[12,192,256]{2,1,0:T(8,128)(2,1)}), bf16[12,192,256]{2,1,0:T(8,128)(2,1)S(1)}, u32[]{:S(2)}, u32[]{:S(2)}) async-start(bf16[12,192,256]{2,1,0:T(8,128)(2,1)} %bitcast.11), calls=%async_computation | async-start | bytes 2359296 | tf_op jit(solution)/shard_map/all_to_all | solution.py:266
  12.0 3.1 %gradients.3 = (bf16[192,3072]{1,0:T(8,128)(2,1)S(1)}, f32[8,128]{1,0:T(8,128)S(1)}, f32[192,256]{1,0:T(8,128)S(1)}, f32[192,256]{1,0:T(8,128)S(1)}) custom-call(f32[8,128]{1,0:T(8,128)S(1)} %get-tuple-element.21.order_ref, bf16[192,3072]{1,0:T(8,128)(2,1)S(1)} %get-tuple-element.22.refs_0_, ...), custom_call_target="tpu_custom_call", output_to_operand_aliasing={{0}: (1, {}), {1}: (2, {}), {2}: (3, {}), {3}: (4, {})} | custom-call | flops 603979776 | bytes 6000000 | tf_op jit(solution)/shard_map/gradients/pallas_call | solution.py:129
  15.1 7.9 %psum.28 = f32[8,128]{1,0:T(8,128)S(1)} all-reduce(f32[8,128]{1,0:T(8,128)S(1)} %get-tuple-element.25), channel_id=1, replica_groups=mesh['x'=4,'zl'=3,'zh'=4,'y'=8,'core'=2] {'core'}, use_global_device_ids=true, to_apply=%region_0.0 | all-reduce | flops 1024 | bytes 8192 | tf_op jit(solution)/shard_map/psum | solution.py:268
  23.0 16.5 %psum.29.total_ref = f32[8,128]{1,0:T(8,128)S(1)} all-reduce(f32[8,128]{1,0:T(8,128)S(1)} %psum.28), channel_id=1, replica_groups={{1,17,33,49},{3,19,35,51},{5,21,37,53},{7,23,39,55},{9,25,41,57},{11,27..., use_global_device_ids=true, to_apply=%region_1.0 | all-reduce | flops 1024 | bytes 8192 | tf_op jit(solution)/shard_map/psum | solution.py:259
  39.5 0.0 all-to-all-done.parts_ref
  39.5 2.0 %update.1 = (bf16[12,192,256]{2,1,0:T(8,128)(2,1)}, f32[192,256]{1,0:T(8,128)}, f32[192,256]{1,0:T(8,128)}, f32[8,128]{1,0:T(8,128)S(1)}) custom-call(bf16[12,192,256]{2,1,0:T(8,128)(2,1)S(1)} %all-to-all-done.parts_ref, f32[8,128]{1,0:T(8,128)S(1)} %psum.29.total_ref, f32[192,256]{1,0:T(8,128)S(1)} %get-tuple-element.26.momentum_ref, ...), custom_call_target="tpu_custom_call" | custom-call | tf_op jit(solution)/shard_map/update/pallas_call | solution.py:193
  41.5 3.8 %all-to-all-start.1 = ((bf16[12,192,256]{2,1,0:T(8,128)(2,1)}), bf16[12,192,256]{2,1,0:T(8,128)(2,1)S(1)}, u32[]{:S(2)}, u32[]{:S(2)}) async-start(bf16[12,192,256]{2,1,0:T(8,128)(2,1)} %get-tuple-element.32), calls=%async_computation.1 | async-start | bytes 2359296 | tf_op jit(solution)/shard_map/all_to_all | solution.py:270
  45.3 1.3 %stage.1 = (bf16[192,3072]{1,0:T(8,128)(2,1)S(1)}, f32[8,128]{1,0:T(8,128)S(1)}) custom-call(f32[8,128]{1,0:T(8,128)S(1)} %get-tuple-element.28.total_ref, bf16[192,3072]{1,0:T(8,128)(2,1)} %bitcast.10), custom_call_target="tpu_custom_call" | custom-call | tf_op jit(solution)/shard_map/stage/pallas_call | solution.py:218
  46.6 14.8 %psum.30 = f32[8,128]{1,0:T(8,128)S(1)} all-reduce(f32[8,128]{1,0:T(8,128)S(1)} %get-tuple-element.29), channel_id=1, replica_groups=mesh['x'=4,'zl'=3,'zh'=4,'y'=8,'core'=2] {'y'}, use_global_device_ids=true, to_apply=%region_2.0 | all-reduce | flops 1024 | bytes 8192 | tf_op jit(solution)/shard_map/psum | solution.py:272
  61.4 2.5 %psum.31.total_ref = f32[8,128]{1,0:T(8,128)S(1)} all-reduce(f32[8,128]{1,0:T(8,128)S(1)} %broadcast_select_fusion), channel_id=1, replica_groups=mesh['x'=4,'zl'=3,'zh'=4,'y'=8,'core'=2] {'core'}, use_global_device_ids=true, to_apply=%region_3.4 | all-reduce | flops 1024 | bytes 8192 | tf_op jit(solution)/shard_map/psum | solution.py:273
  63.9 0.0 all-to-all-done.1.global_ref
  63.9 1.6 %merge.1 = bf16[192,3072]{1,0:T(8,128)(2,1)} custom-call(f32[8,128]{1,0:T(8,128)S(1)} %psum.31.total_ref, bf16[192,3072]{1,0:T(8,128)(2,1)S(1)} %get-tuple-element.30.grads_ref, bf16[192,3072]{1,0:T(8,128)(2,1)S(1)} %get-tuple-element.31.inner_ref, bf16[12,192,256]{2,1,0:T(8,128)(2,1)S(1)} %all-to-all-done.1.global_ref), custom_call_target="tpu_custom_call" | custom-call | tf_op jit(solution)/shard_map/merge/pallas_call | solution.py:245
  (2 shorter events, 0.0 us)
Async XLA Ops:
  3.5 36.0 %all-to-all-start = ((bf16[12,192,256]{2,1,0:T(8,128)(2,1)}), bf16[12,192,256]{2,1,0:T(8,128)(2,1)S(1)}, u32[]{:S(2)}, u32[]{:S(2)}) async-start(bf16[12,192,256]{2,1,0:T(8,128)(2,1)} %bitcast.11), calls=%async_computation | async-start | bytes 2359296 | tf_op jit(solution)/shard_map/all_to_all | solution.py:266
  41.5 22.4 %all-to-all-start.1 = ((bf16[12,192,256]{2,1,0:T(8,128)(2,1)}), bf16[12,192,256]{2,1,0:T(8,128)(2,1)S(1)}, u32[]{:S(2)}, u32[]{:S(2)}) async-start(bf16[12,192,256]{2,1,0:T(8,128)(2,1)} %get-tuple-element.32), calls=%async_computation.1 | async-start | bytes 2359296 | tf_op jit(solution)/shard_map/all_to_all | solution.py:270
